TPU v7x, 1024 devices: a whole 4x8x16 slice. The times are simulated.
1024 devices in a mesh: grp: 64 (over x, z), loc: 16 (over y, core).
Axes of the slice: x: 4, y: 8, z: 16, core: 2. Of those that a mesh axis runs over, the one named last changes fastest.
Arguments:
- inputs: bfloat16 [8192, 2048], P('grp', 'loc'), may hold values from -6 to 6
- out_grad: bfloat16 [8192, 2048], P('grp', 'loc'), may hold values from -6 to 6
- expert_ids: int32 [8192, 10], P('grp'), may hold values from 0 to 511, as said below
- gate_probs: bfloat16 [8192, 10], P('grp'), may hold values from 0.049804688 to 0.5
- group_slot: int32 [8192, 10], P('grp'), may hold values from 0 to 24, as said below
- w_gate: bfloat16 [1024, 2048, 256], P(('grp', 'loc')), may hold values from -0.125 to 0.125
- w_up: bfloat16 [1024, 2048, 256], P(('grp', 'loc')), may hold values from -0.125 to 0.125
- w_down: bfloat16 [1024, 256, 2048], P(('grp', 'loc')), may hold values from -0.25 to 0.25
Outputs:
- in_grad: bfloat16 [8192, 2048], P('grp', 'loc')
- gate_grad: bfloat16 [8192, 10], P('grp')
Inputs may be any that keep to these rules, and one draw needn't show every extreme that they name: `expert_ids`: each row names 10 different experts. `group_slot`: picks of one token into one group share one value. Among the tokens of one grp index bound to one group, the values below 24 number the first of them 0, 1, 2, ... in token order; 24 means the token is not sent to that group.
All inputs are finite; a program needn't handle non-finite values.
Results may differ from a plain program's by a relative error of at most 0.0065.
Values may be sent and summed in bfloat16 or wider, within the bound.
A program may use at most 32 MiB of HBM per device.

v0:
```python
import jax
import jax.numpy as jnp
from jax import lax
from jax.sharding import PartitionSpec as P


def expert_half(rows_x, rows_dy, rows_gate, wg, wu, wd):
    gate_pre = jnp.dot(rows_x, wg, preferred_element_type=jnp.float32)
    up_pre = jnp.dot(rows_x, wu, preferred_element_type=jnp.float32)
    sig = jax.nn.sigmoid(gate_pre)
    act = gate_pre * sig
    back = lax.dot_general(
        rows_dy, wd, (((1,), (1,)), ((), ())), preferred_element_type=jnp.float32
    )
    scaled = rows_gate.astype(jnp.float32)[:, None] * back
    gate_diff = (scaled * up_pre * (sig * (1.0 + gate_pre * (1.0 - sig)))).astype(jnp.bfloat16)
    up_diff = (scaled * act).astype(jnp.bfloat16)
    in_part = lax.dot_general(
        gate_diff, wg, (((1,), (1,)), ((), ())), preferred_element_type=jnp.float32
    )
    in_part = in_part + lax.dot_general(
        up_diff, wu, (((1,), (1,)), ((), ())), preferred_element_type=jnp.float32
    )
    weight_part = jnp.sum(act * up_pre * back, axis=1)
    return (in_part.astype(jnp.bfloat16), weight_part.astype(jnp.bfloat16))


def shards(inputs, out_grad, expert_ids, gate_probs, group_slot, w_gate, w_up, w_down):
    n_grp = lax.axis_size("grp")
    n_loc = lax.axis_size("loc")
    exp_grp = n_loc // 2
    tok_rows, slice_width = inputs.shape
    width = slice_width * n_loc
    room = 2 * tok_rows
    send = max(1, 3 * tok_rows // 16)
    lanes = n_grp * send
    group = expert_ids // exp_grp
    member = expert_ids % exp_grp
    sent = group_slot < send
    lane = group * send + jnp.minimum(group_slot, send - 1)
    hits = jnp.where(sent, lane, lanes)[None] == jnp.arange(lanes, dtype=jnp.int32)[:, None, None]
    place = jnp.any(hits, axis=2).astype(jnp.bfloat16)
    send_x = (
        jnp.dot(place, inputs, preferred_element_type=jnp.float32)
        .astype(jnp.bfloat16)
        .reshape(n_grp, send, slice_width)
    )
    send_dy = (
        jnp.dot(place, out_grad, preferred_element_type=jnp.float32)
        .astype(jnp.bfloat16)
        .reshape(n_grp, send, slice_width)
    )
    spot = jnp.where(sent, lane * exp_grp + member, lanes * exp_grp).reshape(-1)
    marks = (
        jnp.zeros((lanes * exp_grp,), jnp.bfloat16)
        .at[spot]
        .set(gate_probs.reshape(-1), mode="drop")
    )
    marks = marks.reshape(n_grp, send, exp_grp)
    got_x, got_dy, got_marks = (
        lax.all_to_all(send_x, "grp", split_axis=0, concat_axis=0, tiled=True),
        lax.all_to_all(send_dy, "grp", split_axis=0, concat_axis=0, tiled=True),
        lax.all_to_all(marks, "grp", split_axis=0, concat_axis=0, tiled=True),
    )
    flat_marks = got_marks.reshape(lanes, exp_grp)
    picked = flat_marks != 0
    rank = jnp.cumsum(picked.astype(jnp.int32), axis=0) - 1
    live = picked & (rank < room)
    lane_slot = jnp.where(live, rank, room)
    column = jnp.broadcast_to(jnp.arange(exp_grp, dtype=jnp.int32)[None, :], (lanes, exp_grp))
    lane_ids = jnp.broadcast_to(jnp.arange(lanes, dtype=jnp.int32)[:, None], (lanes, exp_grp))
    slot_lane = (
        jnp.full((exp_grp, room), lanes, jnp.int32).at[column, lane_slot].set(lane_ids, mode="drop")
    )
    slot_gate = (
        jnp.zeros((exp_grp, room), jnp.bfloat16).at[column, lane_slot].set(flat_marks, mode="drop")
    )
    blank = jnp.zeros((1, slice_width), jnp.bfloat16)
    fan_x = jnp.concatenate([got_x.reshape(lanes, slice_width), blank], 0)[slot_lane]
    fan_dy = jnp.concatenate([got_dy.reshape(lanes, slice_width), blank], 0)[slot_lane]
    mine = lax.axis_index("loc")
    gates = lax.dynamic_index_in_dim(slot_gate, mine // 2, 0, keepdims=False)
    outgoing_x = jnp.broadcast_to(fan_x[:, None], (exp_grp, 2, room, slice_width)).reshape(
        n_loc, room, slice_width
    )
    outgoing_dy = jnp.broadcast_to(fan_dy[:, None], (exp_grp, 2, room, slice_width)).reshape(
        n_loc, room, slice_width
    )
    rows_x, rows_dy = (
        lax.all_to_all(outgoing_x, "loc", split_axis=0, concat_axis=2, tiled=True),
        lax.all_to_all(outgoing_dy, "loc", split_axis=0, concat_axis=2, tiled=True),
    )
    in_part, weight_part = expert_half(
        rows_x.reshape(room, width),
        rows_dy.reshape(room, width),
        gates,
        w_gate[0],
        w_up[0],
        w_down[0],
    )
    part_g = jnp.broadcast_to(weight_part.reshape(1, room, 1), (1, room, n_loc))
    back_x, back_g = (
        lax.all_to_all(
            in_part.reshape(1, room, n_loc, slice_width),
            "loc",
            split_axis=2,
            concat_axis=0,
            tiled=True,
        ),
        lax.all_to_all(part_g, "loc", split_axis=2, concat_axis=0, tiled=True),
    )
    pair_x = back_x.reshape(exp_grp, 2, room, slice_width).astype(jnp.float32)
    slot_x = pair_x[:, 0] + pair_x[:, 1]
    pair_g = back_g.reshape(exp_grp, 2, room).astype(jnp.float32)
    slot_g = pair_g[:, 0] + pair_g[:, 1]
    padded_x = jnp.concatenate([slot_x, jnp.zeros((exp_grp, 1, slice_width), jnp.float32)], 1)
    padded_g = jnp.concatenate([slot_g, jnp.zeros((exp_grp, 1), jnp.float32)], 1)
    summed = jnp.sum(padded_x[column, lane_slot], axis=1).astype(jnp.bfloat16)
    lane_gate = padded_g[column, lane_slot].astype(jnp.bfloat16)
    home_x, home_g = (
        lax.all_to_all(
            summed.reshape(n_grp, send, slice_width), "grp", split_axis=0, concat_axis=0, tiled=True
        ),
        lax.all_to_all(
            lane_gate.reshape(n_grp, send, exp_grp), "grp", split_axis=0, concat_axis=0, tiled=True
        ),
    )
    in_grad = jnp.einsum(
        "qt,qd->td", place, home_x.reshape(lanes, slice_width), preferred_element_type=jnp.float32
    ).astype(jnp.bfloat16)
    flat_gate = home_g.reshape(-1)
    lookup = jnp.where(sent, lane * exp_grp + member, 0)
    gate_grad = jnp.where(sent, jnp.take(flat_gate, lookup), jnp.zeros((), jnp.bfloat16))
    return (in_grad, gate_grad)


def solution(mesh):
    return jax.shard_map(
        shards,
        mesh=mesh,
        in_specs=(
            P("grp", "loc"),
            P("grp", "loc"),
            P("grp", None),
            P("grp", None),
            P("grp", None),
            P(("grp", "loc"), None, None),
            P(("grp", "loc"), None, None),
            P(("grp", "loc"), None, None),
        ),
        out_specs=(P("grp", "loc"), P("grp", None)),
        check_vma=False,
    )
```

profile of v0, /device:TPU:1, one launch (start us, length us, event | category | flops | bytes accessed | tf_op | source)
XLA Modules:
  0.0 579.2 jit_solution(7281381392879997222)
XLA Ops:
  4.9 12.7 %scatter_custom_fusion = bf16[12288]{0:T(1024)(128)(2,1)S(1)} fusion(s32[1280]{0:T(1024)S(1)} %fusion.36, bf16[1280]{0:T(1024)(128)(2,1)S(1)} %reshape.214, bf16[]{:T(256)} %constant.56.clone.1), kind=kCustom, calls=%fused_computation.77 | custom fusion | bytes 24578 | tf_op jit(solution)/shard_map/scatter | solution.py:57
  18.9 22.8 %all-to-all-start = ((bf16[64,24,8]{1,2,0:T(8,128)(2,1)}), bf16[64,24,8]{1,2,0:T(8,128)(2,1)S(1)}, u32[]{:S(2)}, u32[]{:S(2)}) async-start(bf16[64,24,8]{1,2,0:T(8,128)(2,1)} %copy.83), calls=%async_computation | async-start | bytes 262144 | tf_op jit(solution)/shard_map/all_to_all | solution.py:63
  41.7 1.3 fusion
  43.1 1.8 convolution_convert_fusion
  44.9 10.8 %all-to-all-done = bf16[64,24,8]{1,2,0:T(8,128)(2,1)S(1)} async-done(((bf16[64,24,8]{1,2,0:T(8,128)(2,1)}), bf16[64,24,8]{1,2,0:T(8,128)(2,1)S(1)}, u32[]{:S(2)}, u32[]{:S(2)}) %all-to-all-start) | async-done | bytes 24608 | tf_op jit(solution)/shard_map/all_to_all | solution.py:63
  55.6 7.6 %all-to-all-start.3 = ((bf16[64,24,128]{2,1,0:T(8,128)(2,1)}), bf16[64,24,128]{2,1,0:T(8,128)(2,1)S(1)}, u32[]{:S(2)}, u32[]{:S(2)}) async-start(bf16[64,24,128]{2,1,0:T(8,128)(2,1)} %bitcast.13), calls=%async_computation.3 | async-start | bytes 786432 | tf_op jit(solution)/shard_map/all_to_all | solution.py:61
  63.7 1.8 convolution_convert_fusion.1
  66.0 2.3 reduce-window.6
  68.9 17.8 %all-to-all-done.3 = bf16[64,24,128]{2,1,0:T(8,128)(2,1)S(1)} async-done(((bf16[64,24,128]{2,1,0:T(8,128)(2,1)}), bf16[64,24,128]{2,1,0:T(8,128)(2,1)S(1)}, u32[]{:S(2)}, u32[]{:S(2)}) %all-to-all-start.3) | async-done | bytes 393248 | tf_op jit(solution)/shard_map/all_to_all | solution.py:61
  86.7 9.0 %all-to-all-start.1 = ((bf16[64,24,128]{2,1,0:T(8,128)(2,1)}), bf16[64,24,128]{2,1,0:T(8,128)(2,1)S(1)}, u32[]{:S(2)}, u32[]{:S(2)}) async-start(bf16[64,24,128]{2,1,0:T(8,128)(2,1)} %bitcast.5), calls=%async_computation.1 | async-start | bytes 786432 | tf_op jit(solution)/shard_map/all_to_all | solution.py:62
  96.6 45.4 %scatter_custom_fusion.2 = s32[2048]{0:T(1024)S(1)} fusion(s32[12288]{0:T(1024)S(1)} %reshape.218, s32[12288]{0:T(1024)S(1)} %reshape.226, s32[]{:T(128)} %constant.54.clone.1), kind=kCustom, calls=%fused_computation.84 | custom fusion | bytes 8196
  142.0 6.2 %gather_fusion.1 = bf16[2048,128]{1,0:T(8,128)(2,1)S(1)} fusion(bf16[1537,128]{1,0:T(8,128)(2,1)S(1)} %concatenate.22, s32[2048]{0:T(1024)S(1)} %broadcast_clamp_fusion), kind=kCustom, calls=%fused_computation.1 | custom fusion | bytes 1056768 | tf_op jit(solution)/shard_map/gather | solution.py:79
  149.6 8.8 %all-to-all-start.4 = ((bf16[16,256,128]{1,2,0:T(8,128)(2,1)}), bf16[16,256,128]{1,2,0:T(8,128)(2,1)}, u32[]{:S(2)}, u32[]{:S(2)}) async-start(bf16[16,256,128]{1,2,0:T(8,128)(2,1)} %bitcast.16), calls=%async_computation.4 | async-start | bytes 2097152 | tf_op jit(solution)/shard_map/all_to_all | solution.py:90
  158.5 6.2 %gather_fusion = bf16[2048,128]{1,0:T(8,128)(2,1)S(1)} fusion(bf16[1537,128]{1,0:T(8,128)(2,1)S(1)} %concatenate.21, s32[2048]{0:T(1024)S(1)} %broadcast_clamp_fusion), kind=kCustom, calls=%fused_computation | custom fusion | bytes 1056768 | tf_op jit(solution)/shard_map/gather | solution.py:80
  164.9 21.6 %all-to-all-done.4 = bf16[16,256,128]{1,2,0:T(8,128)(2,1)} async-done(((bf16[16,256,128]{1,2,0:T(8,128)(2,1)}), bf16[16,256,128]{1,2,0:T(8,128)(2,1)}, u32[]{:S(2)}, u32[]{:S(2)}) %all-to-all-start.4) | async-done | bytes 1048608 | tf_op jit(solution)/shard_map/all_to_all | solution.py:90
  187.6 4.2 all-to-all-start.2
  192.5 84.5 %scatter_custom_fusion.1 = bf16[2048]{0:T(1024)(128)(2,1)S(1)} fusion(s32[12288]{0:T(1024)S(1)} %reshape.218, bf16[12288]{0:T(1024)(128)(2,1)S(1)} %reshape.220, bf16[]{:T(256)} %constant.56.clone.1), kind=kCustom, calls=%fused_computation.86 | custom fusion | bytes 4098
  277.0 1.7 fusion.6
  278.8 1.8 fusion.9
  280.5 2.0 multiply_reduce_fusion
  284.4 6.5 %all-to-all-start.7 = ((bf16[16,2,128]{2,1,0:T(2,128)(2,1)}), bf16[16,2,128]{2,1,0:T(2,128)(2,1)S(1)}, u32[]{:S(2)}, u32[]{:S(2)}) async-start(bf16[16,2,128]{2,1,0:T(2,128)(2,1)} %reshape.255), calls=%async_computation.7 | async-start | bytes 16384 | tf_op jit(solution)/shard_map/all_to_all | solution.py:110
  292.2 1.3 copy.91
  293.5 4.4 all-to-all-done.7
  297.9 4.1 all-to-all-start.5
  302.9 100.9 %gather_fusion.3 = bf16[12288]{0:T(1024)(128)(2,1)S(1)} fusion(bf16[8,257]{0,1:T(8,128)(2,1)S(1)} %concatenate.25, s32[12288]{0:T(1024)S(1)} %reshape.190), kind=kCustom, calls=%fused_computation.3 | custom fusion | bytes 147456 | tf_op jit(solution)/shard_map/gather | solution.py:119
  405.2 14.7 %all-to-all-start.8 = ((bf16[64,24,8]{1,2,0:T(8,128)(2,1)}), bf16[64,24,8]{1,2,0:T(8,128)(2,1)S(1)}, u32[]{:S(2)}, u32[]{:S(2)}) async-start(bf16[64,24,8]{1,2,0:T(8,128)(2,1)} %copy.97), calls=%async_computation.8 | async-start | bytes 262144 | tf_op jit(solution)/shard_map/all_to_all | solution.py:124
  420.2 1.2 fusion.3
  421.4 107.9 %gather_fusion.2 = f32[12288,128]{1,0:T(8,128)} fusion(f32[8,257,128]{2,0,1:T(8,128)S(1)} %concatenate.23, s32[12288]{0:T(1024)S(1)} %reshape.190), kind=kCustom, calls=%fused_computation.2 | custom fusion | bytes 12681216 | tf_op jit(solution)/shard_map/gather | solution.py:118
  529.4 10.8 %bitcast_reduce_fusion = bf16[1536,128]{1,0:T(8,128)(2,1)} fusion(f32[12288,128]{1,0:T(8,128)} %gather_fusion.2), kind=kLoop, calls=%fused_computation.10 | loop fusion | flops 1376256 | bytes 6684672 | tf_op jit(solution)/shard_map/reduce_sum | solution.py:118
  540.2 14.6 %all-to-all-start.6 = ((bf16[64,24,128]{2,1,0:T(8,128)(2,1)}), bf16[64,24,128]{2,1,0:T(8,128)(2,1)S(1)}, u32[]{:S(2)}, u32[]{:S(2)}) async-start(bf16[64,24,128]{2,1,0:T(8,128)(2,1)} %bitcast.33), calls=%async_computation.6 | async-start | bytes 786432 | tf_op jit(solution)/shard_map/all_to_all | solution.py:121
  555.6 7.9 %gather_fusion.4 = bf16[1280]{0:T(1024)(128)(2,1)S(1)} fusion(bf16[12288]{0:T(1024)(128)(2,1)S(1)} %reshape.159, s32[2048]{0:T(1024)S(1)} %pad_clamp_fusion), kind=kCustom, calls=%fused_computation.4 | custom fusion | bytes 10240 | tf_op jit(solution)/shard_map/jit(_take)/gather | solution.py:133
  564.4 13.8 %all-to-all-done.6 = bf16[64,24,128]{2,1,0:T(8,128)(2,1)S(1)} async-done(((bf16[64,24,128]{2,1,0:T(8,128)(2,1)}), bf16[64,24,128]{2,1,0:T(8,128)(2,1)S(1)}, u32[]{:S(2)}, u32[]{:S(2)}) %all-to-all-start.6) | async-done | bytes 393248 | tf_op jit(solution)/shard_map/all_to_all | solution.py:121
  (98 shorter events, 19.7 us)
Async XLA Ops:
  0.6 276.4 %copy-start = (bf16[1,2048,256]{2,1,0:T(8,128)(2,1)S(1)}, bf16[1,2048,256]{2,1,0:T(8,128)(2,1)}, u32[]{:S(2)}) copy-start(bf16[1,2048,256]{2,1,0:T(8,128)(2,1)} %param.13) | copy-start | bytes 3145732
  0.6 95.1 %copy-start.10 = (s32[2]{0:T(128)S(1)}, s32[2]{0:T(128)}, u32[]{:S(2)}) copy-start(s32[2]{0:T(128)} %constant.115) | copy-start | bytes 28
  0.7 95.2 %copy-start.9 = (s32[2]{0:T(128)S(1)}, s32[2]{0:T(128)}, u32[]{:S(2)}) copy-start(s32[2]{0:T(128)} %constant.118) | copy-start | bytes 28
  4.0 0.6 copy-start.4
  4.0 0.8 copy-start.7
  18.9 36.8 %all-to-all-start = ((bf16[64,24,8]{1,2,0:T(8,128)(2,1)}), bf16[64,24,8]{1,2,0:T(8,128)(2,1)S(1)}, u32[]{:S(2)}, u32[]{:S(2)}) async-start(bf16[64,24,8]{1,2,0:T(8,128)(2,1)} %copy.83), calls=%async_computation | async-start | bytes 262144 | tf_op jit(solution)/shard_map/all_to_all | solution.py:63
  43.1 98.9 %copy-start.1 = (pred[1536,128]{1,0:T(8,128)(4,1)}, pred[1536,128]{1,0:T(8,128)(4,1)S(1)}, u32[]{:S(2)}) copy-start(pred[1536,128]{1,0:T(8,128)(4,1)S(1)} %fusion) | copy-start | bytes 589828
  55.6 31.1 %all-to-all-start.3 = ((bf16[64,24,128]{2,1,0:T(8,128)(2,1)}), bf16[64,24,128]{2,1,0:T(8,128)(2,1)S(1)}, u32[]{:S(2)}, u32[]{:S(2)}) async-start(bf16[64,24,128]{2,1,0:T(8,128)(2,1)} %bitcast.13), calls=%async_computation.3 | async-start | bytes 786432 | tf_op jit(solution)/shard_map/all_to_all | solution.py:61
  86.7 61.8 %all-to-all-start.1 = ((bf16[64,24,128]{2,1,0:T(8,128)(2,1)}), bf16[64,24,128]{2,1,0:T(8,128)(2,1)S(1)}, u32[]{:S(2)}, u32[]{:S(2)}) async-start(bf16[64,24,128]{2,1,0:T(8,128)(2,1)} %bitcast.5), calls=%async_computation.1 | async-start | bytes 786432 | tf_op jit(solution)/shard_map/all_to_all | solution.py:62
  149.6 36.9 %all-to-all-start.4 = ((bf16[16,256,128]{1,2,0:T(8,128)(2,1)}), bf16[16,256,128]{1,2,0:T(8,128)(2,1)}, u32[]{:S(2)}, u32[]{:S(2)}) async-start(bf16[16,256,128]{1,2,0:T(8,128)(2,1)} %bitcast.16), calls=%async_computation.4 | async-start | bytes 2097152 | tf_op jit(solution)/shard_map/all_to_all | solution.py:90
  158.5 120.3 %copy-start.3 = (bf16[1,2048,256]{2,1,0:T(8,128)(2,1)S(1)}, bf16[1,2048,256]{2,1,0:T(8,128)(2,1)}, u32[]{:S(2)}) copy-start(bf16[1,2048,256]{2,1,0:T(8,128)(2,1)} %param.14) | copy-start | bytes 3145732
  187.6 93.0 %all-to-all-start.2 = ((bf16[16,256,128]{1,2,0:T(8,128)(2,1)}), bf16[16,256,128]{1,2,0:T(8,128)(2,1)}, u32[]{:S(2)}, u32[]{:S(2)}) async-start(bf16[16,256,128]{1,2,0:T(8,128)(2,1)} %bitcast.8), calls=%async_computation.2 | async-start | bytes 2097152 | tf_op jit(solution)/shard_map/all_to_all | solution.py:91
  284.4 13.5 %all-to-all-start.7 = ((bf16[16,2,128]{2,1,0:T(2,128)(2,1)}), bf16[16,2,128]{2,1,0:T(2,128)(2,1)S(1)}, u32[]{:S(2)}, u32[]{:S(2)}) async-start(bf16[16,2,128]{2,1,0:T(2,128)(2,1)} %reshape.255), calls=%async_computation.7 | async-start | bytes 16384 | tf_op jit(solution)/shard_map/all_to_all | solution.py:110
  297.9 107.3 %all-to-all-start.5 = ((bf16[1,256,16,128]{3,1,0,2:T(8,128)(2,1)}), bf16[1,256,16,128]{3,1,0,2:T(8,128)(2,1)S(1)}, u32[]{:S(2)}, u32[]{:S(2)}) async-start(bf16[1,256,16,128]{3,1,0,2:T(8,128)(2,1)} %copy.91), calls=%async_computation.5 | async-start | bytes 2097152 | tf_op jit(solution)/shard_map/all_to_all | solution.py:103
  405.2 135.0 %all-to-all-start.8 = ((bf16[64,24,8]{1,2,0:T(8,128)(2,1)}), bf16[64,24,8]{1,2,0:T(8,128)(2,1)S(1)}, u32[]{:S(2)}, u32[]{:S(2)}) async-start(bf16[64,24,8]{1,2,0:T(8,128)(2,1)} %copy.97), calls=%async_computation.8 | async-start | bytes 262144 | tf_op jit(solution)/shard_map/all_to_all | solution.py:124
  529.4 25.4 %copy-start.6 = (s32[128,10]{1,0:T(8,128)S(1)}, s32[128,10]{1,0:T(8,128)}, u32[]{:S(2)}) copy-start(s32[128,10]{1,0:T(8,128)} %get-tuple-element.10) | copy-start | bytes 15364
  540.2 38.0 %all-to-all-start.6 = ((bf16[64,24,128]{2,1,0:T(8,128)(2,1)}), bf16[64,24,128]{2,1,0:T(8,128)(2,1)S(1)}, u32[]{:S(2)}, u32[]{:S(2)}) async-start(bf16[64,24,128]{2,1,0:T(8,128)(2,1)} %bitcast.33), calls=%async_computation.6 | async-start | bytes 786432 | tf_op jit(solution)/shard_map/all_to_all | solution.py:121
  555.5 8.1 %copy-start.5 = (s32[128,10]{1,0:T(8,128)S(1)}, s32[128,10]{1,0:T(8,128)}, u32[]{:S(2)}) copy-start(s32[128,10]{1,0:T(8,128)} %copy-done.4) | copy-start | bytes 15364
  555.5 8.1 %copy-start.8 = (pred[128,10]{1,0:T(8,128)(4,1)S(1)}, pred[128,10]{1,0:T(8,128)(4,1)}, u32[]{:S(2)}) copy-start(pred[128,10]{1,0:T(8,128)(4,1)} %copy-done.7) | copy-start | bytes 3844
  555.5 22.6 %copy-start.2 = (pred[1536,128]{1,0:T(8,128)(4,1)S(1)}, pred[1536,128]{1,0:T(8,128)(4,1)}, u32[]{:S(2)}) copy-start(pred[1536,128]{1,0:T(8,128)(4,1)} %copy-done.1) | copy-start | bytes 589828
where the time goes:
time: 583 us; the launch traced here: 579 us
  local copies, waits for them, and re-layouts  388 us (67%)
  starting transfers between devices  92.3 us (16%)
  waiting for transfers between devices  68.3 us (12%)
  other arithmetic  17.9 us (3%)
  matrix products  11.1 us (2%)
    unnamed x36, local copies, waits for them, and re-layouts  136 us
    gather x1, local copies, waits for them, and re-layouts, shards(): summed = jnp.sum(padded_x[column, lane_slot], axis=1).astype(jnp.bfloat16)  108 us
    gather x1, local copies, waits for them, and re-layouts, shards(): lane_gate = padded_g[column, lane_slot].astype(jnp.bfloat16)  101 us
    all_to_all x1, starting transfers between devices, shards(): lax.all_to_all(marks, 'grp', split_axis=0, concat_axis=0, tiled=True)  22.8 us
    all_to_all x1, waiting for transfers between devices, shards(): lax.all_to_all(outgoing_x, 'loc', split_axis=0, concat_axis=2, tiled=True)  21.6 us
    all_to_all x1, waiting for transfers between devices, shards(): lax.all_to_all(send_x, 'grp', split_axis=0, concat_axis=0, tiled=True)  17.8 us
    all_to_all x1, starting transfers between devices, shards(): lax.all_to_all(lane_gate.reshape(n_grp, send, exp_grp), 'grp', split_axis...  14.7 us
    all_to_all x1, starting transfers between devices, shards(): lax.all_to_all(summed.reshape(n_grp, send, slice_width), 'grp', split_axi...  14.6 us
  transfers between devices with their start and end apart: 9, of which 5 were waited for; matrix products, arithmetic and copies ran while one was open for 68% of the time, Pallas kernels for 0%

commit v1 on v0

v1 whole, which is shorter than its diff:
```python
import jax
import jax.numpy as jnp
from jax import lax
from jax.sharding import PartitionSpec as P

F32 = jnp.float32
BF16 = jnp.bfloat16
I32 = jnp.int32


def dot(a, b):
    return jnp.dot(a, b, preferred_element_type=F32)


def expert_half(rows_x, rows_dy, rows_gate, wg, wu, wd):
    g = dot(rows_x, wg)
    u = dot(rows_x, wu)
    b = lax.dot_general(rows_dy, wd, (((1,), (1,)), ((), ())), preferred_element_type=F32)
    s = jax.nn.sigmoid(g)
    a = g * s
    q = rows_gate.astype(F32)[:, None] * b
    dg = (q * u * (s * (1.0 + g * (1.0 - s)))).astype(BF16)
    du = (q * a).astype(BF16)
    part = lax.dot_general(dg, wg, (((1,), (1,)), ((), ())), preferred_element_type=F32)
    part = part + lax.dot_general(du, wu, (((1,), (1,)), ((), ())), preferred_element_type=F32)
    return part, jnp.sum(a * u * b, axis=1)


def shards(inputs, out_grad, expert_ids, gate_probs, group_slot, w_gate, w_up, w_down):
    n_grp = lax.axis_size("grp")
    n_loc = lax.axis_size("loc")
    exp_grp = n_loc // 2
    tok, wide = inputs.shape
    room = 2 * tok
    send = max(1, 3 * tok // 16)
    lanes = n_grp * send
    meta = 256
    pad = meta // exp_grp
    c_rows = room // wide
    core = lax.axis_index("loc") % 2
    mine = lax.axis_index("loc") // 2

    group = expert_ids // exp_grp
    member = expert_ids % exp_grp
    sent = group_slot < send
    lane = jnp.where(sent, group * send + group_slot, lanes)
    place = jnp.any(
        lane.T[None] == jnp.arange(lanes, dtype=I32)[:, None, None], axis=1
    ).astype(BF16)
    field = jnp.where(sent, member * pad + group_slot, meta).reshape(-1)
    of_group = (group.reshape(-1)[None, :] == jnp.arange(n_grp, dtype=I32)[:, None]).astype(BF16)
    of_field = field[:, None] == jnp.arange(meta, dtype=I32)[None, :]
    marks = dot(
        of_group, jnp.where(of_field, gate_probs.reshape(-1)[:, None], jnp.zeros((), BF16))
    ).astype(BF16)
    both = jnp.concatenate([inputs, out_grad], 1)
    packed = dot(place, both).astype(BF16).reshape(n_grp, send, 2 * wide)
    outgoing = jnp.concatenate(
        [packed[:, :, :wide], packed[:, :, wide:], marks.reshape(n_grp, meta // wide, wide)], 1
    )
    got = lax.all_to_all(outgoing, "grp", split_axis=0, concat_axis=0, tiled=True)

    rows = jnp.concatenate([got[:, :send], got[:, send : 2 * send]], 2).reshape(lanes, 2 * wide)
    got_marks = got[:, 2 * send :].reshape(n_grp, meta)
    picked = got_marks != 0
    count = picked.astype(BF16)
    f_row = jnp.arange(meta, dtype=I32)[:, None]
    f_col = jnp.arange(meta, dtype=I32)[None, :]
    same = f_row // pad == f_col // pad
    within = dot(count, (same & (f_row <= f_col)).astype(BF16))
    total = dot(count, same.astype(BF16)).astype(BF16)
    earlier = (
        jnp.arange(n_grp, dtype=I32)[None, :] < jnp.arange(n_grp, dtype=I32)[:, None]
    ).astype(BF16)
    rank = within + dot(earlier, total) - 1.0
    rank = jnp.where(picked & (rank < room), rank, 2.0 * room).astype(I32)
    by_lane = rank.reshape(n_grp, exp_grp, pad)[:, :, :send].transpose(1, 0, 2).reshape(exp_grp, lanes)
    gate_lane = (
        got_marks.reshape(n_grp, exp_grp, pad)[:, :, :send].transpose(1, 0, 2).reshape(exp_grp, lanes)
    )
    pick_of = (by_lane[:, None, :] == jnp.arange(room, dtype=I32)[None, :, None]).astype(BF16)
    fan = dot(pick_of.reshape(exp_grp * room, lanes), rows).astype(BF16)
    fan = fan.reshape(exp_grp, room, 2 * wide)
    my_rank = lax.dynamic_index_in_dim(by_lane, mine, 0, keepdims=False)
    my_gate = lax.dynamic_index_in_dim(gate_lane, mine, 0, keepdims=False)
    my_pick = my_rank[None, :] == jnp.arange(room, dtype=I32)[:, None]
    gates = jnp.sum(jnp.where(my_pick, my_gate.astype(F32)[None, :], 0.0), axis=1)

    same_core = [[2 * y + c for y in range(exp_grp)] for c in range(2)]
    swap = [(i, i ^ 1) for i in range(n_loc)]
    own = lax.all_to_all(
        fan, "loc", split_axis=0, concat_axis=0, axis_index_groups=same_core, tiled=True
    )
    other = lax.ppermute(own, "loc", swap)
    low = jnp.where(core == 0, own, other)
    high = jnp.where(core == 0, other, own)
    full = jnp.stack([low, high], 1).reshape(n_loc, room, 2, wide).transpose(2, 1, 0, 3)
    full = full.reshape(2, room, n_loc * wide)
    part, c_part = expert_half(full[0], full[1], gates, w_gate[0], w_up[0], w_down[0])

    blocks = part.reshape(room, exp_grp, 2, wide).transpose(2, 1, 0, 3)
    keep = jnp.where(core == 0, blocks[0], blocks[1])
    give = jnp.where(core == 0, blocks[1], blocks[0]).astype(BF16)
    given = lax.ppermute(give, "loc", swap).astype(F32)
    c_given = lax.ppermute(c_part.astype(BF16), "loc", swap).astype(F32)
    pair_x = (keep + given).astype(BF16)
    pair_c = (c_part.astype(BF16).astype(F32) + c_given).astype(BF16)
    pair_c = jnp.broadcast_to(pair_c.reshape(1, c_rows, wide), (exp_grp, c_rows, wide))
    back = lax.all_to_all(
        jnp.concatenate([pair_x, pair_c], 1),
        "loc",
        split_axis=0,
        concat_axis=0,
        axis_index_groups=same_core,
        tiled=True,
    )
    slot_x = back[:, :room].reshape(exp_grp * room, wide)
    slot_c = back[:, room:].reshape(exp_grp, room)
    summed = lax.dot_general(
        pick_of.reshape(exp_grp * room, lanes),
        slot_x,
        (((0,), (0,)), ((), ())),
        preferred_element_type=F32,
    ).astype(BF16)
    lane_c = jnp.einsum("mr,mrl->ml", slot_c, pick_of, preferred_element_type=F32).astype(BF16)
    home_c = jnp.pad(
        lane_c.reshape(exp_grp, n_grp, send).transpose(1, 0, 2), ((0, 0), (0, 0), (0, pad - send))
    ).reshape(n_grp, meta // wide, wide)
    home = lax.all_to_all(
        jnp.concatenate([summed.reshape(n_grp, send, wide), home_c], 1),
        "grp",
        split_axis=0,
        concat_axis=0,
        tiled=True,
    )
    in_grad = lax.dot_general(
        place,
        home[:, :send].reshape(lanes, wide),
        (((0,), (0,)), ((), ())),
        preferred_element_type=F32,
    ).astype(BF16)
    table = home[:, send:].reshape(n_grp, meta)
    picks = lax.dot_general(
        of_group, table, (((0,), (0,)), ((), ())), preferred_element_type=F32
    )
    gate_grad = jnp.sum(jnp.where(of_field, picks, 0.0), axis=1).astype(BF16)
    return in_grad, gate_grad.reshape(expert_ids.shape)


def solution(mesh):
    return jax.shard_map(
        shards,
        mesh=mesh,
        in_specs=(
            P("grp", "loc"),
            P("grp", "loc"),
            P("grp", None),
            P("grp", None),
            P("grp", None),
            P(("grp", "loc"), None, None),
            P(("grp", "loc"), None, None),
            P(("grp", "loc"), None, None),
        ),
        out_specs=(P("grp", "loc"), P("grp", None)),
        check_vma=False,
    )
```

time: 583 us -> 206 us (0.35)
  local copies, waits for them, and re-layouts: 388 us -> 11.9 us
  blocking collectives: 0 us -> 89.6 us
  starting transfers between devices: 92.3 us -> 35.1 us
  waiting for transfers between devices: 68.3 us -> 46.3 us
  other arithmetic: 17.9 us -> 5.8 us
    gather x8 -> x0, local copies, waits for them, and re-layouts: 230 us -> none  [the longest x1 108 us: shards(): summed = jnp.sum(padded_x[column, lane_slot], axis=1).astype(jnp.bfloat16)]
    unnamed x36 -> x13, local copies, waits for them, and re-layouts: 136 us -> 2.37 us
    all_to_all x0 -> x3, blocking collectives: none -> 89.6 us  [the longest x1 38.6 us: shards(): lax.all_to_all(jnp.concatenate([summed.reshape(n_grp, send, wide), home_c...]
    all_to_all x9 -> x1, starting transfers between devices: 92.3 us -> 22.8 us  [shards(): lax.all_to_all(outgoing, 'grp', split_axis=0, concat_axis=0, tiled=True)]
    all_to_all x9 -> x1, waiting for transfers between devices: 68.3 us -> 45.5 us  [shards(): lax.all_to_all(outgoing, 'grp', split_axis=0, concat_axis=0, tiled=True)]
    scatter x3 -> x0, local copies, waits for them, and re-layouts: 12.7 us -> none  [the longest x1 12.7 us: shards(): marks = jnp.zeros((lanes * exp_grp,), jnp.bfloat16).at[spot].set(gate_pro...]
    ppermute x0 -> x3, starting transfers between devices: none -> 12.3 us  [the longest x1 7.99 us: shards(): other = lax.ppermute(own, 'loc', swap)]
    reduce_sum x1, other arithmetic: 10.8 us -> 0.24 us  [shards(): jnp.sum(jnp.where(my_pick, my_gate.astype(F32)[None, :], 0.0), axis=1)]
  transfers between devices with their start and end apart: 9 -> 4, of which waited for: 5 -> 2; matrix products, arithmetic and copies ran while one was open for 68% -> 1% of each run, Pallas kernels for 0% -> 0%
where the time goes in v1:
time: 206 us; the launch traced here: 203 us
  blocking collectives  89.6 us (43%)
  waiting for transfers between devices  46.3 us (22%)
  starting transfers between devices  35.1 us (17%)
  matrix products  13.4 us (7%)
  local copies, waits for them, and re-layouts  11.9 us (6%)
  other arithmetic  5.8 us (3%)
    all_to_all x1, waiting for transfers between devices, shards(): lax.all_to_all(outgoing, 'grp', split_axis=0, concat_axis=0, tiled=True)  45.5 us
    all_to_all x1, blocking collectives, shards(): lax.all_to_all(jnp.concatenate([summed.reshape(n_grp, send, wide), home_c...  38.6 us
    all_to_all x1, blocking collectives, shards(): lax.all_to_all(fan, 'loc', split_axis=0, concat_axis=0, axis_index_groups...  30.4 us
    all_to_all x1, starting transfers between devices, shards(): lax.all_to_all(outgoing, 'grp', split_axis=0, concat_axis=0, tiled=True)  22.8 us
    all_to_all x1, blocking collectives, shards(): lax.all_to_all(jnp.concatenate([pair_x, pair_c], 1), 'loc', split_axis=0,...  20.7 us
    ppermute x1, starting transfers between devices, shards(): other = lax.ppermute(own, 'loc', swap)  7.99 us
    reshape x2, local copies, waits for them, and re-layouts, shards(): blocks = part.reshape(room, exp_grp, 2, wide).transpose(2, 1, 0, 3)  5.11 us
    dot_general x7, matrix products, dot(): return jnp.dot(a, b, preferred_element_type=F32)  5.05 us
  transfers between devices with their start and end apart: 4, of which 2 were waited for; matrix products, arithmetic and copies ran while one was open for 1% of the time, Pallas kernels for 0%

profile of v1, /device:TPU:1, one launch (start us, length us, event | category | flops | bytes accessed | tf_op | source)
XLA Modules:
  0.0 203.2 jit_solution(1160383282020408269)
XLA Ops:
  0.6 0.9 copy.78
  1.7 0.7 fusion.59
  3.3 1.3 fusion
  4.6 1.1 convolution_convert_fusion.1
  5.9 1.0 pad_maximum_fusion.1
  7.0 22.8 %all-to-all-start = ((bf16[64,50,128]{2,1,0:T(8,128)(2,1)}), bf16[64,50,128]{2,1,0:T(8,128)(2,1)S(1)}, u32[]{:S(2)}, u32[]{:S(2)}) async-start(bf16[64,50,128]{2,1,0:T(8,128)(2,1)} %pad_maximum_fusion.1), calls=%async_computation | async-start | bytes 1835008 | tf_op jit(solution)/shard_map/all_to_all | solution.py:61
  29.8 45.5 %all-to-all-done = bf16[64,50,128]{2,1,0:T(8,128)(2,1)S(1)} async-done(((bf16[64,50,128]{2,1,0:T(8,128)(2,1)}), bf16[64,50,128]{2,1,0:T(8,128)(2,1)S(1)}, u32[]{:S(2)}, u32[]{:S(2)}) %all-to-all-start) | async-done | bytes 819232 | tf_op jit(solution)/shard_map/all_to_all | solution.py:61
  76.3 1.7 iota_compare_fusion
  78.1 1.9 convolution_convert_fusion
  80.0 0.5 copy.85
  80.5 30.4 %all_to_all.20 = bf16[8,256,256]{1,2,0:T(8,128)(2,1)S(1)} all-to-all(bf16[8,256,256]{1,2,0:T(8,128)(2,1)S(1)} %copy.85), channel_id=1, replica_groups={{0,2,4,6,8,10,12,14},{1,3,5,7,9,11,13,15},{16,18,20,22,24,26,28,30},{17..., dimensions={0} | all-to-all | bytes 2097152 | tf_op jit(solution)/shard_map/all_to_all | solution.py:91
  111.0 8.0 %collective-permute-start = (bf16[8,256,256]{1,2,0:T(8,128)(2,1)S(1)}, bf16[8,256,256]{1,2,0:T(8,128)(2,1)S(1)}, u32[]{:S(2)}, u32[]{:S(2)}) collective-permute-start(bf16[8,256,256]{1,2,0:T(8,128)(2,1)S(1)} %all_to_all.20), channel_id=1, source_target_pairs={{0,1},{1,0},{2,3},{3,2},{4,5},{5,4},{6,7},{7,6},{8,9},{9,8},{10,11... | collective-permute-start | bytes 3145736 | tf_op jit(solution)/shard_map/ppermute | solution.py:94
  119.1 0.6 slice_bitcast_fusion.1
  119.7 0.9 copy.84
  121.7 0.5 fusion.13
  122.2 0.6 copy-done.1
  122.9 0.5 fusion.16
  123.4 0.5 multiply_reduce_fusion
  123.9 0.6 fusion.11
  124.5 0.5 convolution_add_fusion
  125.0 2.8 %reshape.187 = f32[256,8,2,128]{3,2,1,0:T(2,128)} reshape(f32[256,2048]{1,0:T(8,128)S(1)} %convolution_add_fusion) | data formatting | bytes 4194304 | tf_op jit(solution)/shard_map/reshape | solution.py:101
  127.8 2.3 %copy.121 = f32[256,8,2,128]{3,0,1,2:T(8,128)S(1)} copy(f32[256,8,2,128]{3,2,1,0:T(2,128)} %reshape.187) | data formatting | bytes 4194304 | tf_op jit(solution)/shard_map/reshape | solution.py:101
  130.2 2.2 %collective-permute-start.1 = (bf16[8,256,128]{2,1,0:T(8,128)(2,1)S(1)}, bf16[8,256,128]{2,1,0:T(8,128)(2,1)S(1)}, u32[]{:S(2)}, u32[]{:S(2)}) collective-permute-start(bf16[8,256,128]{2,1,0:T(8,128)(2,1)S(1)} %fusion.22), channel_id=1, source_target_pairs={{0,1},{1,0},{2,3},{3,2},{4,5},{5,4},{6,7},{7,6},{8,9},{9,8},{10,11... | collective-permute-start | bytes 1572872 | tf_op jit(solution)/shard_map/ppermute | solution.py:104
  132.4 2.2 %collective-permute-start.2 = (bf16[256]{0:T(256)(128)(2,1)S(1)}, bf16[256]{0:T(256)(128)(2,1)S(1)}, u32[]{:S(2)}, u32[]{:S(2)}) collective-permute-start(bf16[256]{0:T(256)(128)(2,1)S(1)} %get-tuple-element.23), channel_id=1, source_target_pairs={{0,1},{1,0},{2,3},{3,2},{4,5},{5,4},{6,7},{7,6},{8,9},{9,8},{10,11... | collective-permute-start | bytes 1544 | tf_op jit(solution)/shard_map/ppermute | solution.py:105
  134.6 0.8 collective-permute-done.2
  135.6 20.7 %all_to_all.21 = bf16[8,258,128]{2,1,0:T(8,128)(2,1)S(1)} all-to-all(bf16[8,258,128]{2,1,0:T(8,128)(2,1)S(1)} %pad_maximum_fusion.3), channel_id=1, replica_groups={{0,2,4,6,8,10,12,14},{1,3,5,7,9,11,13,15},{16,18,20,22,24,26,28,30},{17..., dimensions={0} | all-to-all | bytes 1056768 | tf_op jit(solution)/shard_map/all_to_all | solution.py:109
  156.3 2.0 fusion.1
  158.7 3.4 %fusion.6 = bf16[1536,128]{1,0:T(8,128)(2,1)S(1)} fusion(s32[8,1536]{1,0:T(8,128)S(1)} %eq.126, bf16[8,258,128]{2,1,0:T(8,128)(2,1)S(1)} %all_to_all.21), kind=kOutput, calls=%fused_computation.12 | convolution fusion | flops 808648704 | bytes 966656 | tf_op jit(solution)/shard_map/dot_general | solution.py:119
  162.2 38.6 %all_to_all.22 = bf16[64,26,128]{2,1,0:T(8,128)(2,1)S(1)} all-to-all(bf16[64,26,128]{2,1,0:T(8,128)(2,1)S(1)} %pad_maximum_fusion.4), channel_id=1, replica_groups=mesh['grp'=64,'loc'=16] {'grp'}, dimensions={0} | all-to-all | bytes 851968 | tf_op jit(solution)/shard_map/all_to_all | solution.py:129
  200.9 1.0 convolution_convert_fusion.4
  201.9 0.4 fusion.8
  202.5 0.7 copy.91
  (53 shorter events, 4.5 us)
Async XLA Ops:
  0.6 121.0 %copy-start = (bf16[1,2048,256]{2,1,0:T(8,128)(2,1)S(1)}, bf16[1,2048,256]{2,1,0:T(8,128)(2,1)}, u32[]{:S(2)}) copy-start(bf16[1,2048,256]{2,1,0:T(8,128)(2,1)} %param.13) | copy-start | bytes 3145732
  2.9 4.0 %copy-start.2 = (s32[1280]{0:T(1024)}, s32[1280]{0:T(1024)S(1)}, u32[]{:S(2)}) copy-start(s32[1280]{0:T(1024)S(1)} %eq.115) | copy-start | bytes 15364
  7.0 68.3 %all-to-all-start = ((bf16[64,50,128]{2,1,0:T(8,128)(2,1)}), bf16[64,50,128]{2,1,0:T(8,128)(2,1)S(1)}, u32[]{:S(2)}, u32[]{:S(2)}) async-start(bf16[64,50,128]{2,1,0:T(8,128)(2,1)} %pad_maximum_fusion.1), calls=%async_computation | async-start | bytes 1835008 | tf_op jit(solution)/shard_map/all_to_all | solution.py:61
  111.0 10.2 %collective-permute-start = (bf16[8,256,256]{1,2,0:T(8,128)(2,1)S(1)}, bf16[8,256,256]{1,2,0:T(8,128)(2,1)S(1)}, u32[]{:S(2)}, u32[]{:S(2)}) collective-permute-start(bf16[8,256,256]{1,2,0:T(8,128)(2,1)S(1)} %all_to_all.20), channel_id=1, source_target_pairs={{0,1},{1,0},{2,3},{3,2},{4,5},{5,4},{6,7},{7,6},{8,9},{9,8},{10,11... | collective-permute-start | bytes 3145736 | tf_op jit(solution)/shard_map/ppermute | solution.py:94
  121.7 1.2 copy-start.1
  121.7 1.8 copy-start.4
  130.2 5.2 %collective-permute-start.1 = (bf16[8,256,128]{2,1,0:T(8,128)(2,1)S(1)}, bf16[8,256,128]{2,1,0:T(8,128)(2,1)S(1)}, u32[]{:S(2)}, u32[]{:S(2)}) collective-permute-start(bf16[8,256,128]{2,1,0:T(8,128)(2,1)S(1)} %fusion.22), channel_id=1, source_target_pairs={{0,1},{1,0},{2,3},{3,2},{4,5},{5,4},{6,7},{7,6},{8,9},{9,8},{10,11... | collective-permute-start | bytes 1572872 | tf_op jit(solution)/shard_map/ppermute | solution.py:104
  132.4 3.0 %collective-permute-start.2 = (bf16[256]{0:T(256)(128)(2,1)S(1)}, bf16[256]{0:T(256)(128)(2,1)S(1)}, u32[]{:S(2)}, u32[]{:S(2)}) collective-permute-start(bf16[256]{0:T(256)(128)(2,1)S(1)} %get-tuple-element.23), channel_id=1, source_target_pairs={{0,1},{1,0},{2,3},{3,2},{4,5},{5,4},{6,7},{7,6},{8,9},{9,8},{10,11... | collective-permute-start | bytes 1544 | tf_op jit(solution)/shard_map/ppermute | solution.py:105
  162.2 39.7 %copy-start.3 = (s32[1280]{0:T(1024)S(1)}, s32[1280]{0:T(1024)}, u32[]{:S(2)}) copy-start(s32[1280]{0:T(1024)} %copy-done.2) | copy-start | bytes 15364

commit v2 on v1

v2 whole, which is shorter than its diff:
```python
import jax
import jax.numpy as jnp
from jax import lax
from jax.experimental import pallas as pl
from jax.experimental.pallas import tpu as pltpu
from jax.sharding import PartitionSpec as P

MESH = pl.DeviceIdType.MESH

F32 = jnp.float32
BF16 = jnp.bfloat16
I32 = jnp.int32


def dot(a, b):
    return jnp.dot(a, b, preferred_element_type=F32)


def ring_offset(i, n):
    half = (i + 1) // 2
    return n // 2 + jnp.where(i % 2 == 0, half, -half)


def middle_kernel(
    rows_ref, rank_row, rank_col, gate_ref, wg_ref, wu_ref, wd_ref,
    out_x, out_c,
    fan_x, fan_dy, full_x, full_dy, acc_g, acc_u, acc_b, dg_ref, du_ref,
    keep, give, got, pair, back, c_own, c_got, c_all, acc,
    fan_ss, fan_rs, twin_ss, twin_rs, give_ss, give_rs, ret_ss, ret_rs,
    cx_ss, cx_rs, cr_ss, cr_rs,
):
    n = full_x.shape[0]
    room, wide = fan_x.shape[1:]
    lanes = rows_ref.shape[0]
    grp = lax.axis_index("grp")
    loc = lax.axis_index("loc")
    y, core = loc // 2, loc % 2
    twin = (grp, 2 * y + 1 - core)
    my_cols = pl.ds(pl.multiple_of(core * wide, wide), wide)

    def peer(yy):
        return (grp, 2 * yy + core)

    def rdma(src, dst, ss, rs, to):
        return pltpu.make_async_remote_copy(
            src_ref=src, dst_ref=dst, send_sem=ss, recv_sem=rs, device_id=to, device_id_type=MESH
        )

    def fan_copy(m, slot, k):
        src, dst = ((fan_dy, full_dy), (fan_x, full_x))[k]
        return rdma(
            src.at[m], dst.at[slot, :, my_cols], fan_ss.at[m, k], fan_rs.at[slot, k], peer(m)
        )

    def twin_copy(slot, k):
        buf = (full_dy, full_x)[k]
        return rdma(
            buf.at[slot, :, my_cols], buf.at[slot, :, my_cols],
            twin_ss.at[slot, k], twin_rs.at[slot, k], twin,
        )

    def twin_arrival(slot, k):
        buf = (full_dy, full_x)[k]
        cols = pl.ds(pl.multiple_of((1 - core) * wide, wide), wide)
        return rdma(
            buf.at[slot, :, cols], buf.at[slot, :, cols],
            twin_ss.at[slot, k], twin_rs.at[slot, k], twin,
        )

    barrier = pltpu.get_barrier_semaphore()

    def greet(i, _):
        pl.semaphore_signal(barrier, inc=1, device_id=peer((y + i) % n), device_id_type=MESH)
        return _

    lax.fori_loop(1, n, greet, 0)
    pl.semaphore_signal(barrier, inc=1, device_id=twin, device_id_type=MESH)
    pl.semaphore_wait(barrier, n)

    slot_iota = lax.broadcasted_iota(I32, (room, lanes), 0).astype(F32)

    def spread(i, _):
        m = (y + ring_offset(i, n)) % n
        pick = (rank_row[m] == slot_iota).astype(F32).astype(BF16)
        block = dot(pick, rows_ref[...]).astype(BF16)

        @pl.when(i < n - 1)
        def _far():
            fan_x[m] = block[:, :wide]
            fan_dy[m] = block[:, wide:]
            fan_copy(m, y, 0).start()
            fan_copy(m, y, 1).start()

        @pl.when(i == n - 1)
        def _near():
            full_x[y, :, my_cols] = block[:, :wide]
            full_dy[y, :, my_cols] = block[:, wide:]
            twin_copy(y, 0).start()
            twin_copy(y, 1).start()

        return _

    lax.fori_loop(0, n, spread, 0)

    acc_g[...] = jnp.zeros_like(acc_g)
    acc_u[...] = jnp.zeros_like(acc_u)
    acc_b[...] = jnp.zeros_like(acc_b)

    def source(i):
        return (y + n - ring_offset(i, n)) % n

    def multiply(slot):
        twin_arrival(slot, 0).wait_recv()
        twin_arrival(slot, 1).wait_recv()
        rows = pl.ds(pl.multiple_of(slot * 2 * wide, 2 * wide), 2 * wide)
        xs = full_x[slot]
        acc_b[...] += lax.dot_general(
            full_dy[slot], wd_ref[:, rows], (((1,), (1,)), ((), ())), preferred_element_type=F32
        )
        acc_g[...] += dot(xs, wg_ref[rows, :])
        acc_u[...] += dot(xs, wu_ref[rows, :])

    def gather(i, _):
        slot = source(i)
        fan_copy(slot, slot, 0).wait_recv()
        twin_copy(slot, 0).start()
        fan_copy(slot, slot, 1).wait_recv()
        twin_copy(slot, 1).start()
        multiply(jnp.where(i == 0, y, source(jnp.maximum(i - 1, 0))))
        return _

    lax.fori_loop(0, n - 1, gather, 0)
    multiply(source(n - 2))

    g = acc_g[...]
    u = acc_u[...]
    b = acc_b[...]
    s = 1.0 / (1.0 + jnp.exp(-g))
    a = g * s
    q = gate_ref[...] * b
    dg_ref[...] = (q * u * (s * (1.0 + g * (1.0 - s)))).astype(BF16)
    du_ref[...] = (q * a).astype(BF16)
    gate_part = a * u * b
    high = gate_part.astype(BF16)
    low = (gate_part - high.astype(F32)).astype(BF16)
    ones = jnp.ones((8, gate_part.shape[1]), BF16)
    nt = (((1,), (1,)), ((), ()))
    c_half = lax.dot_general(ones, high, nt, preferred_element_type=F32) + lax.dot_general(
        ones, low, nt, preferred_element_type=F32
    )
    c_own[...] = c_half.astype(BF16).astype(F32)
    rdma(c_own, c_got, cx_ss, cx_rs, twin).start()

    def give_copy(t):
        return rdma(give.at[t], got.at[t], give_ss.at[t], give_rs.at[t], twin)

    def ret_copy(t, slot):
        return rdma(pair.at[t], back.at[slot], ret_ss.at[t], ret_rs.at[slot], peer(t))

    def c_copy(t, slot):
        return rdma(c_all.at[y], c_all.at[slot], cr_ss.at[t], cr_rs.at[slot], peer(t))

    def target(i):
        return (y + ring_offset(i, n)) % n

    def add_pair(i):
        t = target(i)
        give_copy(t).wait_recv()
        total = (keep[t] + got[t].astype(F32)).astype(BF16)

        @pl.when(i < n - 1)
        def _far():
            pair[t] = total
            ret_copy(t, y).start()

        @pl.when(i == n - 1)
        def _near():
            back[y] = total

    def produce(i, _):
        t = target(i)
        rows = pl.ds(pl.multiple_of(t * 2 * wide, 2 * wide), 2 * wide)
        part = lax.dot_general(dg_ref[...], wg_ref[rows, :], nt, preferred_element_type=F32)
        part = part + lax.dot_general(du_ref[...], wu_ref[rows, :], nt, preferred_element_type=F32)
        left, right = part[:, :wide], part[:, wide:]
        keep[t] = jnp.where(core == 0, left, right)
        give[t] = jnp.where(core == 0, right, left).astype(BF16)
        give_copy(t).start()

        @pl.when(i > 0)
        def _before():
            add_pair(jnp.maximum(i - 1, 0))

        return _

    lax.fori_loop(0, n, produce, 0)
    add_pair(n - 1)

    rdma(c_own, c_got, cx_ss, cx_rs, twin).wait_recv()
    c_all[y] = (c_own[...] + c_got[...]).astype(BF16).astype(F32)

    def c_send(i, _):
        c_copy(target(i), y).start()
        return _

    lax.fori_loop(0, n - 1, c_send, 0)

    acc[...] = jnp.zeros_like(acc)
    lane_iota = lax.broadcasted_iota(I32, (lanes, room), 1).astype(F32)
    eye = lax.broadcasted_iota(I32, (room, room), 0) == lax.broadcasted_iota(I32, (room, room), 1)
    col_iota = lax.broadcasted_iota(I32, (room, wide), 1)
    pick_row = lax.broadcasted_iota(I32, (wide, room), 0)

    def combine(slot):
        rank = dot(rank_col[...], (pick_row == slot).astype(F32).astype(BF16))
        pick = (rank == lane_iota).astype(F32).astype(BF16)
        c_col = jnp.sum(jnp.where(eye, c_all[slot][:1, :], 0.0), axis=1, keepdims=True)
        c_cols = jnp.where(col_iota == slot, c_col, 0.0).astype(BF16)
        acc[...] += dot(pick, jnp.concatenate([back[slot], c_cols], axis=1))

    combine(y)

    def collect(i, _):
        slot = source(i)
        ret_copy(slot, slot).wait_recv()
        c_copy(slot, slot).wait_recv()
        combine(slot)
        return _

    lax.fori_loop(0, n - 1, collect, 0)
    out_x[...] = acc[:, :wide].astype(BF16)
    out_c[...] = acc[:, wide:].astype(BF16)

    def drain(i, _):
        t = target(i)
        fan_copy(t, y, 0).wait_send()
        fan_copy(t, y, 1).wait_send()
        ret_copy(t, y).wait_send()
        c_copy(t, y).wait_send()
        return _

    lax.fori_loop(0, n - 1, drain, 0)

    def drain_twin(i, _):
        twin_copy(i, 0).wait_send()
        twin_copy(i, 1).wait_send()
        give_copy(i).wait_send()
        return _

    lax.fori_loop(0, n, drain_twin, 0)
    rdma(c_own, c_got, cx_ss, cx_rs, twin).wait_send()


def middle(rows, rank_row, rank_col, gates, wg, wu, wd):
    lanes = rows.shape[0]
    n, room, wide = rank_row.shape[0], gates.shape[0], rows.shape[1] // 2
    hidden = wg.shape[1]
    dma = pltpu.SemaphoreType.DMA
    block = (n, room, wide)
    vmem = pl.BlockSpec(memory_space=pltpu.VMEM)
    return pl.pallas_call(
        middle_kernel,
        out_shape=(
            jax.ShapeDtypeStruct((lanes, wide), BF16),
            jax.ShapeDtypeStruct((lanes, wide), BF16),
        ),
        in_specs=[vmem] * 7,
        out_specs=(vmem, vmem),
        scratch_shapes=[
            pltpu.VMEM(block, BF16),
            pltpu.VMEM(block, BF16),
            pltpu.VMEM((n, room, 2 * wide), BF16),
            pltpu.VMEM((n, room, 2 * wide), BF16),
            pltpu.VMEM((room, hidden), F32),
            pltpu.VMEM((room, hidden), F32),
            pltpu.VMEM((room, hidden), F32),
            pltpu.VMEM((room, hidden), BF16),
            pltpu.VMEM((room, hidden), BF16),
            pltpu.VMEM(block, F32),
            pltpu.VMEM(block, BF16),
            pltpu.VMEM(block, BF16),
            pltpu.VMEM(block, BF16),
            pltpu.VMEM(block, BF16),
            pltpu.VMEM((8, room), F32),
            pltpu.VMEM((8, room), F32),
            pltpu.VMEM((n, 8, room), F32),
            pltpu.VMEM((lanes, 2 * wide), F32),
            dma((n, 2)),
            dma((n, 2)),
            dma((n, 2)),
            dma((n, 2)),
            dma((n,)),
            dma((n,)),
            dma((n,)),
            dma((n,)),
            dma,
            dma,
            dma((n,)),
            dma((n,)),
        ],
        compiler_params=pltpu.CompilerParams(
            collective_id=0, has_side_effects=True, vmem_limit_bytes=40 << 20
        ),
        cost_estimate=pl.CostEstimate(
            flops=10 * room * hidden * n * 2 * wide, bytes_accessed=8 << 20, transcendentals=0
        ),
    )(rows, rank_row, rank_col, gates, wg, wu, wd)


def shards(inputs, out_grad, expert_ids, gate_probs, group_slot, w_gate, w_up, w_down):
    n_grp = lax.axis_size("grp")
    n_loc = lax.axis_size("loc")
    exp_grp = n_loc // 2
    tok, wide = inputs.shape
    room = 2 * tok
    send = max(1, 3 * tok // 16)
    lanes = n_grp * send
    meta = 256
    pad = meta // exp_grp
    mine = lax.axis_index("loc") // 2

    group = expert_ids // exp_grp
    member = expert_ids % exp_grp
    sent = group_slot < send
    lane = jnp.where(sent, group * send + group_slot, lanes)
    place = jnp.any(
        lane.T[None] == jnp.arange(lanes, dtype=I32)[:, None, None], axis=1
    ).astype(BF16)
    field = jnp.where(sent, member * pad + group_slot, meta).reshape(-1)
    of_group = (group.reshape(-1)[None, :] == jnp.arange(n_grp, dtype=I32)[:, None]).astype(BF16)
    of_field = field[:, None] == jnp.arange(meta, dtype=I32)[None, :]
    marks = dot(
        of_group, jnp.where(of_field, gate_probs.reshape(-1)[:, None], jnp.zeros((), BF16))
    ).astype(BF16)
    both = jnp.concatenate([inputs, out_grad], 1)
    packed = dot(place, both).astype(BF16).reshape(n_grp, send, 2 * wide)
    outgoing = jnp.concatenate(
        [packed[:, :, :wide], packed[:, :, wide:], marks.reshape(n_grp, meta // wide, wide)], 1
    )
    got = lax.all_to_all(outgoing, "grp", split_axis=0, concat_axis=0, tiled=True)

    rows = jnp.concatenate([got[:, :send], got[:, send : 2 * send]], 2).reshape(lanes, 2 * wide)
    got_marks = got[:, 2 * send :].reshape(n_grp, meta)
    picked = got_marks != 0
    count = picked.astype(BF16)
    f_row = jnp.arange(meta, dtype=I32)[:, None]
    f_col = jnp.arange(meta, dtype=I32)[None, :]
    same = f_row // pad == f_col // pad
    within = dot(count, (same & (f_row <= f_col)).astype(BF16))
    total = dot(count, same.astype(BF16)).astype(BF16)
    earlier = (
        jnp.arange(n_grp, dtype=I32)[None, :] < jnp.arange(n_grp, dtype=I32)[:, None]
    ).astype(BF16)
    rank = within + dot(earlier, total) - 1.0
    rank = jnp.where(picked & (rank < room), rank, 2.0 * room).astype(I32)
    by_lane = rank.reshape(n_grp, exp_grp, pad)[:, :, :send].transpose(1, 0, 2).reshape(exp_grp, lanes)
    gate_lane = (
        got_marks.reshape(n_grp, exp_grp, pad)[:, :, :send].transpose(1, 0, 2).reshape(exp_grp, lanes)
    )
    my_rank = lax.dynamic_index_in_dim(by_lane, mine, 0, keepdims=False)
    my_gate = lax.dynamic_index_in_dim(gate_lane, mine, 0, keepdims=False)
    my_pick = my_rank[None, :] == jnp.arange(room, dtype=I32)[:, None]
    gates = jnp.sum(jnp.where(my_pick, my_gate.astype(F32)[None, :], 0.0), axis=1, keepdims=True)
    summed, lane_c = middle(
        rows,
        by_lane.astype(F32).reshape(exp_grp, 1, lanes),
        jnp.pad(by_lane.astype(BF16).T, ((0, 0), (0, wide - exp_grp))),
        gates,
        w_gate[0],
        w_up[0],
        w_down[0],
    )
    lane_c = lane_c[:, :exp_grp].T
    home_c = jnp.pad(
        lane_c.reshape(exp_grp, n_grp, send).transpose(1, 0, 2), ((0, 0), (0, 0), (0, pad - send))
    ).reshape(n_grp, meta // wide, wide)
    home = lax.all_to_all(
        jnp.concatenate([summed.reshape(n_grp, send, wide), home_c], 1),
        "grp",
        split_axis=0,
        concat_axis=0,
        tiled=True,
    )
    in_grad = lax.dot_general(
        place,
        home[:, :send].reshape(lanes, wide),
        (((0,), (0,)), ((), ())),
        preferred_element_type=F32,
    ).astype(BF16)
    table = home[:, send:].reshape(n_grp, meta)
    picks = lax.dot_general(
        of_group, table, (((0,), (0,)), ((), ())), preferred_element_type=F32
    )
    gate_grad = jnp.sum(jnp.where(of_field, picks, 0.0), axis=1).astype(BF16)
    return in_grad, gate_grad.reshape(expert_ids.shape)


def solution(mesh):
    return jax.shard_map(
        shards,
        mesh=mesh,
        in_specs=(
            P("grp", "loc"),
            P("grp", "loc"),
            P("grp", None),
            P("grp", None),
            P("grp", None),
            P(("grp", "loc"), None, None),
            P(("grp", "loc"), None, None),
            P(("grp", "loc"), None, None),
        ),
        out_specs=(P("grp", "loc"), P("grp", None)),
        check_vma=False,
    )
```

time: 206 us -> 179 us (0.87)
  Pallas kernels: 0 us -> 56.1 us
  blocking collectives: 89.6 us -> 37.9 us
  starting transfers between devices: 35.1 us -> 22.8 us
  matrix products: 13.4 us -> 2.74 us
  local copies, waits for them, and re-layouts: 11.9 us -> 6.52 us
  other arithmetic: 5.8 us -> 3.56 us
    pallas_call x0 -> x1, Pallas kernels: none -> 56.1 us  [middle(): pl.pallas_call(middle_kernel, out_shape=(jax.ShapeDtypeStruct((lanes, wid...]
    all_to_all x2 -> x0, blocking collectives: 51.1 us -> none  [the longest x1 30.4 us: shards(): lax.all_to_all(fan, 'loc', split_axis=0, concat_axis=0, axis_index_groups...]
    ppermute x3 -> x0, starting transfers between devices: 12.3 us -> none  [the longest x1 7.99 us: shards(): other = lax.ppermute(own, 'loc', swap)]
    dot_general x5 -> x0, matrix products: 6.95 us -> none  [the longest x1 3.44 us: shards(): lax.dot_general(pick_of.reshape(exp_grp * room, lanes), slot_x, (((0,), (...]
    reshape x4 -> x0, local copies, waits for them, and re-layouts: 5.65 us -> none  [the longest x2 5.11 us: shards(): blocks = part.reshape(room, exp_grp, 2, wide).transpose(2, 1, 0, 3)]
    dot_general x7 -> x4, matrix products: 5.05 us -> 1.32 us  [dot(): return jnp.dot(a, b, preferred_element_type=F32)]
  transfers between devices with their start and end apart: 4 -> 1, of which waited for: 2 -> 1; matrix products, arithmetic and copies ran while one was open for 1% -> 0% of each run, Pallas kernels for 0% -> 0%
where the time goes in v2:
time: 179 us; the launch traced here: 176 us
  Pallas kernels  56.1 us (31%)
  waiting for transfers between devices  45.4 us (25%)
  blocking collectives  37.9 us (21%)
  starting transfers between devices  22.8 us (13%)
  local copies, waits for them, and re-layouts  6.52 us (4%)
  other arithmetic  3.56 us (2%)
  matrix products  2.74 us (2%)
    pallas_call x1, Pallas kernels, middle(): pl.pallas_call(middle_kernel, out_shape=(jax.ShapeDtypeStruct((lanes, wid...  56.1 us
    all_to_all x1, waiting for transfers between devices, shards(): lax.all_to_all(outgoing, 'grp', split_axis=0, concat_axis=0, tiled=True)  45.4 us
    all_to_all x1, blocking collectives, shards(): lax.all_to_all(jnp.concatenate([summed.reshape(n_grp, send, wide), home_c...  37.9 us
    all_to_all x1, starting transfers between devices, shards(): lax.all_to_all(outgoing, 'grp', split_axis=0, concat_axis=0, tiled=True)  22.8 us
  transfers between devices with their start and end apart: 1, of which 1 were waited for; matrix products, arithmetic and copies ran while one was open for 0% of the time, Pallas kernels for 0%

profile of v2, /device:TPU:1, one launch (start us, length us, event | category | flops | bytes accessed | tf_op | source)
XLA Modules:
  0.0 176.1 jit_solution(13534263974619469956)
XLA Ops:
  0.6 0.8 copy.59
  1.5 0.1 broadcast_in_dim.62
  1.6 0.7 fusion.36
  2.5 0.1 eq.86
  2.7 0.1 eq.82
  2.9 0.3 convolution_convert_fusion.2
  3.2 1.3 fusion
  4.6 0.4 convolution_convert_fusion
  4.9 0.1 fusion.43
  5.1 1.0 pad_maximum_fusion
  6.1 22.8 %all-to-all-start = ((bf16[64,50,128]{2,1,0:T(8,128)(2,1)}), bf16[64,50,128]{2,1,0:T(8,128)(2,1)S(1)}, u32[]{:S(2)}, u32[]{:S(2)}) async-start(bf16[64,50,128]{2,1,0:T(8,128)(2,1)} %pad_maximum_fusion), calls=%async_computation | async-start | bytes 1835008 | tf_op jit(solution)/shard_map/all_to_all | solution.py:340
  28.9 45.4 %all-to-all-done = bf16[64,50,128]{2,1,0:T(8,128)(2,1)S(1)} async-done(((bf16[64,50,128]{2,1,0:T(8,128)(2,1)}), bf16[64,50,128]{2,1,0:T(8,128)(2,1)S(1)}, u32[]{:S(2)}, u32[]{:S(2)}) %all-to-all-start) | async-done | bytes 819232 | tf_op jit(solution)/shard_map/all_to_all | solution.py:340
  74.5 0.2 fusion.10
  74.8 0.4 select_convert_fusion
  75.3 0.1 copy.66
  75.4 0.2 reshape.138
  75.6 0.1 copy.63
  75.7 0.2 convert_element_type.60.rank_row
  75.9 0.3 copy.64
  76.4 0.5 dynamic-slice_reduce_fusion
  76.9 0.2 select_reduce_fusion
  77.1 0.1 copy.68.gate_ref
  77.6 0.9 copy-done.2
  78.5 0.3 copy-done
  78.8 0.3 copy-done.1
  79.1 56.1 %shard_map.95 = (bf16[1536,128]{1,0:T(8,128)(2,1)S(1)}, bf16[1536,128]{1,0:T(8,128)(2,1)S(1)}) custom-call(bf16[1536,256]{1,0:T(8,128)(2,1)S(1)} %bitcast.53, f32[8,1,1536]{2,1,0:T(1,128)S(1)} %convert_element_type.60.rank_row, bf16[1536,128]{1,0:T(8,128)(2,1)S(1)} %pad.8.rank_col, f32[256,1]{1,0:T(8,128)S(1)} %copy.68.gate_ref, ...), custom_call_target="tpu_custom_call" | custom-call | flops 1342177280 | bytes 8388608 | tf_op jit(solution)/shard_map/pallas_call | solution.py:261
  135.3 0.3 copy.69
  135.8 37.9 %all_to_all.10 = bf16[64,26,128]{2,1,0:T(8,128)(2,1)S(1)} all-to-all(bf16[64,26,128]{2,1,0:T(8,128)(2,1)S(1)} %pad_maximum_fusion.2), channel_id=1, replica_groups=mesh['grp'=64,'loc'=16] {'grp'}, dimensions={0} | all-to-all | bytes 851968 | tf_op jit(solution)/shard_map/all_to_all | solution.py:377
  173.8 1.0 convolution_convert_fusion.3
  174.8 0.4 fusion.2
  175.2 0.2 convert_element_type.59
  175.4 0.7 copy.71
  (26 shorter events, 1.1 us)
Async XLA Ops:
  0.6 3.9 %copy-start.3 = (bf16[128,128]{1,0:T(8,128)(2,1)S(1)}, bf16[128,128]{1,0:T(8,128)(2,1)}, u32[]{:S(2)}) copy-start(bf16[128,128]{1,0:T(8,128)(2,1)} %param.9) | copy-start | bytes 98308
  0.6 3.9 %copy-start.4 = (bf16[128,128]{1,0:T(8,128)(2,1)S(1)}, bf16[128,128]{1,0:T(8,128)(2,1)}, u32[]{:S(2)}) copy-start(bf16[128,128]{1,0:T(8,128)(2,1)} %param.8) | copy-start | bytes 98308
  6.1 68.3 %all-to-all-start = ((bf16[64,50,128]{2,1,0:T(8,128)(2,1)}), bf16[64,50,128]{2,1,0:T(8,128)(2,1)S(1)}, u32[]{:S(2)}, u32[]{:S(2)}) async-start(bf16[64,50,128]{2,1,0:T(8,128)(2,1)} %pad_maximum_fusion), calls=%async_computation | async-start | bytes 1835008 | tf_op jit(solution)/shard_map/all_to_all | solution.py:340
  77.3 1.2 copy-start.2
  77.4 1.5 copy-start
  77.4 1.8 %copy-start.1 = (bf16[1,2048,256]{2,1,0:T(8,128)(2,1)S(1)}, bf16[1,2048,256]{2,1,0:T(8,128)(2,1)}, u32[]{:S(2)}) copy-start(bf16[1,2048,256]{2,1,0:T(8,128)(2,1)} %param.14) | copy-start | bytes 3145732

commit v3 on v2

v3 whole, which is shorter than its diff:
```python
import jax
import jax.numpy as jnp
from jax import lax
from jax.experimental import pallas as pl
from jax.experimental.pallas import tpu as pltpu
from jax.sharding import PartitionSpec as P

MESH = pl.DeviceIdType.MESH
F32 = jnp.float32
BF16 = jnp.bfloat16
I32 = jnp.int32
NX = 4
META = 256
NT = (((1,), (1,)), ((), ()))


def dot(a, b):
    return jnp.dot(a, b, preferred_element_type=F32)


def bits(mask):
    return mask.astype(F32).astype(BF16)


def ring_offset(i, n):
    half = (i + 1) // 2
    return n // 2 + jnp.where(i % 2 == 0, half, -half)


def near_offset(i, n):
    half = (i + 1) // 2
    return jnp.where(i % 2 == 0, n - half, half) % n


def kernel(
    sx_ref, sdy_ref, marks_ref, wg_hbm, wu_hbm, wd_hbm,
    out_x, out_c,
    wg_ref, wu_ref, wd_ref,
    z_dy, z_x, z_marks, x_dy, x_x, l_dy, l_x, l_marks, pick_ref, rank_ref,
    fan_x, fan_dy, full_x, full_dy, acc_g, acc_u, acc_b, dg_ref, du_ref,
    keep, give, got, pair, back, c_own, c_got, c_all, acc,
    o_x, m_x, h_x, o_c, m_c, s_c, h_c, zo_x,
    w_sem, z_ss, z_rs, x_ss, x_rs, xm_ss, xm_rs,
    fan_ss, fan_rs, twin_ss, twin_rs, give_ss, give_rs, ret_ss, ret_rs,
    cx_ss, cx_rs, cr_ss, cr_rs, hx_ss, hx_rs, hc_ss, hc_rs, hz_ss, hz_rs,
):
    n = full_x.shape[0]
    room, wide = fan_x.shape[1:]
    nz, chunk = z_x.shape[:2]
    send = chunk // NX
    two = 2 * send
    pairs = nz // 2
    lanes = nz * chunk
    n_grp = NX * nz
    pad = META // n
    half = META // 2
    grp = lax.axis_index("grp")
    loc = lax.axis_index("loc")
    x, z = grp // nz, grp % nz
    y, core = loc // 2, loc % 2
    twin = (grp, 2 * y + 1 - core)
    my_cols = pl.ds(pl.multiple_of(core * wide, wide), wide)
    twin_cols = pl.ds(pl.multiple_of((1 - core) * wide, wide), wide)

    def rdma(src, dst, ss, rs, to):
        return pltpu.make_async_remote_copy(
            src_ref=src, dst_ref=dst, send_sem=ss, recv_sem=rs, device_id=to, device_id_type=MESH
        )

    def at_z(zz):
        return (x * nz + zz, loc)

    def at_x(xx):
        return (xx * nz + z, loc)

    def peer(yy):
        return (grp, 2 * yy + core)

    loads = [
        pltpu.make_async_copy(src, dst, w_sem.at[i])
        for i, (src, dst) in enumerate(((wg_hbm, wg_ref), (wu_hbm, wu_ref), (wd_hbm, wd_ref)))
    ]
    for load in loads:
        load.start()

    barrier = pltpu.get_barrier_semaphore()

    def greet(to):
        pl.semaphore_signal(barrier, inc=1, device_id=to, device_id_type=MESH)

    def greet_z(i, _):
        greet(at_z((z + i) % nz))
        return _

    def greet_y(i, _):
        greet(peer((y + i) % n))
        return _

    lax.fori_loop(1, nz, greet_z, 0)
    for dx in range(1, NX):
        greet(at_x((x + dx) % NX))
    lax.fori_loop(1, n, greet_y, 0)
    greet(twin)
    pl.semaphore_wait(barrier, nz - 1 + NX - 1 + n - 1 + 1)

    def eight(slot):
        return pl.ds(pl.multiple_of(slot * 8, 8), 8)

    def z_copy(k, to, slot):
        src = (marks_ref, sdy_ref, sx_ref)[k].at[to]
        dst = (z_marks.at[eight(slot)], z_dy.at[slot], z_x.at[slot])[k]
        return rdma(src, dst, z_ss.at[k, to], z_rs.at[k, slot], at_z(to))

    for k in range(3):

        def z_send(i, _, k=k):
            z_copy(k, (z + ring_offset(i, nz)) % nz, z).start()
            return _

        lax.fori_loop(0, nz - 1, z_send, 0)

    z_marks[eight(z)] = marks_ref[z]
    z_dy[z] = sdy_ref[z]
    z_x[z] = sx_ref[z]

    def all_z(slot):
        return pl.ds(pl.multiple_of(slot * nz * 8, 8), nz * 8)

    def marks_copy(to, slot):
        return rdma(z_marks, l_marks.at[all_z(slot)], xm_ss.at[to], xm_rs.at[slot], at_x(to))

    def marks_in(i, _):
        z_copy(0, (z + i) % nz, (z + i) % nz).wait_recv()
        return _

    lax.fori_loop(1, nz, marks_in, 0)
    for dx in range(1, NX):
        marks_copy((x + dx) % NX, x).start()
    l_marks[all_z(x)] = z_marks[...]

    def pair_rows(j):
        return pl.ds(pl.multiple_of(j * two, 16 if two % 16 == 0 else 1), two)

    def x_copy(k, to, slot, j):
        src, dst = ((x_dy, l_dy), (x_x, l_x))[k]
        rows = pair_rows(j)
        return rdma(
            src.at[to, rows], dst.at[slot, rows], x_ss.at[k, to, j], x_rs.at[k, slot, j], at_x(to)
        )

    def onward(k, i):
        src, out, land = ((z_dy, x_dy, l_dy), (z_x, x_x, l_x))[k]
        j = (z // 2 + near_offset(i, pairs)) % pairs
        for zz in range(2):
            slot = 2 * j + zz

            @pl.when(slot != z)
            def _arrival():
                z_copy(1 + k, slot, slot).wait_recv()

        even = src[2 * j].astype(F32)
        odd = src[2 * j + 1].astype(F32)
        rows = pair_rows(j)
        for xx in range(NX):
            part = slice(xx * send, (xx + 1) * send)
            both = jnp.concatenate([even[part], odd[part]], axis=0).astype(BF16)

            @pl.when(xx != x)
            def _far():
                out[xx, rows] = both
                x_copy(k, xx, x, j).start()

            @pl.when(xx == x)
            def _near():
                land[xx, rows] = both

    def onward_dy(i, _):
        onward(0, i)
        return _

    lax.fori_loop(0, pairs, onward_dy, 0)

    for dx in range(1, NX):
        marks_copy((x + dx) % NX, (x + dx) % NX).wait_recv()
    f_row = lax.broadcasted_iota(I32, (half, half), 0)
    f_col = lax.broadcasted_iota(I32, (half, half), 1)
    same = f_row // pad == f_col // pad
    upto = bits(same & (f_row <= f_col))
    block = bits(same)
    earlier = bits(
        lax.broadcasted_iota(I32, (n_grp, n_grp), 1) < lax.broadcasted_iota(I32, (n_grp, n_grp), 0)
    )
    lane_of = lax.broadcasted_iota(I32, (lanes, n_grp), 0)
    src_of = lax.broadcasted_iota(I32, (lanes, n_grp), 1) * send
    from_src = bits((lane_of >= src_of) & (lane_of < src_of + send))
    lane_f = lax.broadcasted_iota(I32, (lanes, half), 0)
    col_f = lax.broadcasted_iota(I32, (lanes, half), 1)
    slot_of = (col_f % pad) == (lane_f % send)
    rank_cols = jnp.zeros((lanes, wide), F32)
    gate_cols = jnp.zeros((lanes, wide), F32)
    per = half // pad
    for ab in range(2):
        marks = l_marks[pl.ds(2 * x + ab, n_grp, 8), :]
        picked = marks != 0.0
        count = bits(picked)
        within = dot(count, upto)
        before = dot(earlier, dot(count, block).astype(BF16))
        rank = within + before - 1.0
        rank = jnp.where(picked & (rank < room), rank, 2.0 * room).astype(BF16)
        fold_row = lax.broadcasted_iota(I32, (half, wide), 0)
        fold_col = lax.broadcasted_iota(I32, (half, wide), 1)
        fold = bits(fold_row // pad + ab * per == fold_col)
        ranks = jnp.where(slot_of, dot(from_src, rank), 0.0).astype(BF16)
        gates = jnp.where(slot_of, dot(from_src, marks.astype(BF16)), 0.0).astype(BF16)
        rank_cols = rank_cols + dot(ranks, fold)
        gate_cols = gate_cols + dot(gates, fold)
    rank_ref[...] = rank_cols.astype(BF16)
    gate_cols = gate_cols.astype(BF16)
    rank_rows = rank_cols.T[:8]
    slot_iota = lax.broadcasted_iota(I32, (room, lanes), 0).astype(F32)
    for m in range(n):
        pick_ref[m] = bits(rank_rows[m : m + 1, :] == slot_iota)
    gate_slots = dot(pick_ref[y], gate_cols)
    my_lane = lax.broadcasted_iota(I32, (room, wide), 1) == y
    gate_col = jnp.sum(jnp.where(my_lane, gate_slots, 0.0), axis=1, keepdims=True)

    def fan_copy(k, m, slot):
        src, dst = ((fan_dy, full_dy), (fan_x, full_x))[k]
        return rdma(
            src.at[m], dst.at[slot, :, my_cols], fan_ss.at[m, k], fan_rs.at[slot, k], peer(m)
        )

    def twin_copy(k, slot):
        buf = (full_dy, full_x)[k]
        return rdma(
            buf.at[slot, :, my_cols], buf.at[slot, :, my_cols],
            twin_ss.at[slot, k], twin_rs.at[slot, k], twin,
        )

    def twin_arrival(k, slot):
        buf = (full_dy, full_x)[k]
        return rdma(
            buf.at[slot, :, twin_cols], buf.at[slot, :, twin_cols],
            twin_ss.at[slot, k], twin_rs.at[slot, k], twin,
        )

    def landed(k):
        land = (l_dy, l_x)[k]

        def wait(i, _):
            for dx in range(1, NX):
                xx = (x + dx) % NX
                x_copy(k, xx, xx, i).wait_recv()
            return _

        lax.fori_loop(0, pairs, wait, 0)
        return land[...].reshape(lanes, wide)

    def spread(k):
        src, dst, rows = ((fan_dy, full_dy), (fan_x, full_x))[k] + (landed(k),)

        def one(i, _):
            m = (y + ring_offset(i, n)) % n
            out = dot(pick_ref[m], rows).astype(BF16)

            @pl.when(i < n - 1)
            def _far():
                src[m] = out
                fan_copy(k, m, y).start()

            @pl.when(i == n - 1)
            def _near():
                dst[y, :, my_cols] = out
                twin_copy(k, y).start()

            return _

        lax.fori_loop(0, n, one, 0)

    def source(i):
        return (y + n - ring_offset(i, n)) % n

    def hand_over(k, i):
        slot = source(i)
        fan_copy(k, slot, slot).wait_recv()
        twin_copy(k, slot).start()

    def columns(slot):
        return pl.ds(pl.multiple_of(slot * 2 * wide, 2 * wide), 2 * wide)

    spread(0)
    acc_g[...] = jnp.zeros_like(acc_g)
    acc_u[...] = jnp.zeros_like(acc_u)
    acc_b[...] = jnp.zeros_like(acc_b)

    def onward_x(i, _):
        onward(1, i)

        @pl.when(i < n - 1)
        def _dy():
            hand_over(0, jnp.minimum(i, n - 2))

        return _

    lax.fori_loop(0, pairs, onward_x, 0)
    for i in range(pairs, n - 1):
        hand_over(0, i)
    spread(1)
    loads[2].wait()

    def back_rows(slot, _):
        twin_arrival(0, slot).wait_recv()
        acc_b[...] += lax.dot_general(
            full_dy[slot], wd_ref[:, columns(slot)], NT, preferred_element_type=F32
        )
        return _

    lax.fori_loop(0, n, back_rows, 0)
    loads[0].wait()
    loads[1].wait()

    def multiply(slot):
        twin_arrival(1, slot).wait_recv()
        rows = columns(slot)
        xs = full_x[slot]
        acc_g[...] += dot(xs, wg_ref[rows, :])
        acc_u[...] += dot(xs, wu_ref[rows, :])

    def gather(i, _):
        hand_over(1, i)
        multiply(jnp.where(i == 0, y, source(jnp.maximum(i - 1, 0))))
        return _

    lax.fori_loop(0, n - 1, gather, 0)
    multiply(source(n - 2))

    g = acc_g[...]
    u = acc_u[...]
    b = acc_b[...]
    s = 1.0 / (1.0 + jnp.exp(-g))
    a = g * s
    q = gate_col * b
    dg_ref[...] = (q * u * (s * (1.0 + g * (1.0 - s)))).astype(BF16)
    du_ref[...] = (q * a).astype(BF16)
    gate_part = a * u * b
    high = gate_part.astype(BF16)
    low = (gate_part - high.astype(F32)).astype(BF16)
    ones = jnp.ones((8, gate_part.shape[1]), BF16)
    c_half = lax.dot_general(ones, high, NT, preferred_element_type=F32) + lax.dot_general(
        ones, low, NT, preferred_element_type=F32
    )
    c_own[...] = c_half.astype(BF16).astype(F32)
    rdma(c_own, c_got, cx_ss, cx_rs, twin).start()

    def give_copy(t):
        return rdma(give.at[t], got.at[t], give_ss.at[t], give_rs.at[t], twin)

    def ret_copy(t, slot):
        return rdma(pair.at[t], back.at[slot], ret_ss.at[t], ret_rs.at[slot], peer(t))

    def c_copy(t, slot):
        return rdma(c_all.at[y], c_all.at[slot], cr_ss.at[t], cr_rs.at[slot], peer(t))

    def target(i):
        return (y + ring_offset(i, n)) % n

    def add_pair(i):
        t = target(i)
        give_copy(t).wait_recv()
        total = (keep[t] + got[t].astype(F32)).astype(BF16)

        @pl.when(i < n - 1)
        def _far():
            pair[t] = total
            ret_copy(t, y).start()

        @pl.when(i == n - 1)
        def _near():
            back[y] = total

    def produce(i, _):
        t = target(i)
        rows = pl.ds(pl.multiple_of(t * 2 * wide, 2 * wide), 2 * wide)
        part = lax.dot_general(dg_ref[...], wg_ref[rows, :], NT, preferred_element_type=F32)
        part = part + lax.dot_general(du_ref[...], wu_ref[rows, :], NT, preferred_element_type=F32)
        left, right = part[:, :wide], part[:, wide:]
        keep[t] = jnp.where(core == 0, left, right)
        give[t] = jnp.where(core == 0, right, left).astype(BF16)
        give_copy(t).start()

        @pl.when(i > 0)
        def _before():
            add_pair(jnp.maximum(i - 1, 0))

        return _

    lax.fori_loop(0, n, produce, 0)
    rdma(c_own, c_got, cx_ss, cx_rs, twin).wait_recv()
    c_all[y] = (c_own[...] + c_got[...]).astype(BF16).astype(F32)

    def c_send(i, _):
        c_copy(target(i), y).start()
        return _

    lax.fori_loop(0, n - 1, c_send, 0)

    add_pair(n - 1)

    acc[...] = jnp.zeros_like(acc)
    lane_iota = lax.broadcasted_iota(I32, (lanes, room), 1).astype(F32)
    eye = lax.broadcasted_iota(I32, (room, room), 0) == lax.broadcasted_iota(I32, (room, room), 1)
    col_iota = lax.broadcasted_iota(I32, (room, wide), 1)
    pick_row = lax.broadcasted_iota(I32, (wide, room), 0)

    def combine(slot):
        rank = dot(rank_ref[...], bits(pick_row == slot))
        pick = bits(rank == lane_iota)
        c_col = jnp.sum(jnp.where(eye, c_all[slot][:1, :], 0.0), axis=1, keepdims=True)
        c_cols = jnp.where(col_iota == slot, c_col, 0.0).astype(BF16)
        acc[...] += dot(pick, jnp.concatenate([back[slot], c_cols], axis=1))

    combine(y)

    def collect(i, _):
        slot = source(i)
        ret_copy(slot, slot).wait_recv()
        c_copy(slot, slot).wait_recv()
        combine(slot)
        return _

    lax.fori_loop(0, n - 1, collect, 0)

    total = acc[:, :wide].astype(BF16).reshape(NX, nz * send, wide)
    lane_c = acc[:, wide:].astype(BF16)
    un_row = lax.broadcasted_iota(I32, (wide, half), 0)
    un_col = lax.broadcasted_iota(I32, (wide, half), 1)
    lane_to = lax.broadcasted_iota(I32, (n_grp, lanes), 1)
    src_to = lax.broadcasted_iota(I32, (n_grp, lanes), 0) * send
    to_src = bits((lane_to >= src_to) & (lane_to < src_to + send))

    def home_x(to, slot):
        return rdma(o_x.at[to], m_x.at[slot], hx_ss.at[to], hx_rs.at[slot], at_x(to))

    def both_z(slot):
        return pl.ds(pl.multiple_of(slot * 2 * nz, 8), 2 * nz)

    def home_c(to, slot):
        return rdma(o_c.at[to], m_c.at[both_z(slot)], hc_ss.at[to], hc_rs.at[slot], at_x(to))

    for xx in range(NX):

        @pl.when(xx != x)
        def _far():
            o_x[xx] = total[xx]
            home_x(xx, x).start()

        @pl.when(xx == x)
        def _near():
            m_x[xx] = total[xx]

    for ab in range(2):
        spread_c = dot(lane_c, bits(un_col // pad + ab * per == un_row))
        table = dot(to_src, jnp.where(slot_of, spread_c, 0.0).astype(BF16))
        for xx in range(NX):
            o_c[xx, ab * nz : (ab + 1) * nz, :] = table[xx * nz : (xx + 1) * nz]
    for dx in range(1, NX):
        home_c((x + dx) % NX, x).start()
    m_c[both_z(x)] = o_c[x]
    for dx in range(1, NX):
        xx = (x + dx) % NX
        home_x(xx, xx).wait_recv()
        home_c(xx, xx).wait_recv()

    def home_z(k, to, slot):
        src, dst = ((zo_x, h_x), (s_c, h_c))[k]
        return rdma(src.at[to], dst.at[slot], hz_ss.at[k, to], hz_rs.at[k, slot], at_z(to))

    def off(i, _):
        j = (z // 2 + ring_offset(i, pairs)) % pairs
        rows = pair_rows(j)
        parts = [m_x[xx, rows].astype(F32) for xx in range(NX)]
        for zz in range(2):
            to = 2 * j + zz
            zo_x[to] = jnp.concatenate(
                [part[zz * send : (zz + 1) * send] for part in parts], axis=0
            ).astype(BF16)
            for ab in range(2):
                s_c[to, ab * NX : (ab + 1) * NX, :] = m_c[
                    pl.ds(ab * nz + to, NX, 2 * nz), :
                ]

            @pl.when(to != z)
            def _far():
                home_z(0, to, z).start()
                home_z(1, to, z).start()

        return _

    lax.fori_loop(0, pairs, off, 0)
    h_x[z] = zo_x[z]
    h_c[z] = s_c[z]

    def home_in(i, _):
        slot = (z + i) % nz
        home_z(0, slot, slot).wait_recv()
        home_z(1, slot, slot).wait_recv()
        return _

    lax.fori_loop(1, nz, home_in, 0)
    out_x[...] = h_x[...]
    out_c[...] = h_c[...]

    def drain_z(i, _):
        to = (z + i) % nz
        for k in range(3):
            z_copy(k, to, z).wait_send()
        home_z(0, to, z).wait_send()
        home_z(1, to, z).wait_send()
        return _

    lax.fori_loop(1, nz, drain_z, 0)
    for dx in range(1, NX):
        to = (x + dx) % NX
        marks_copy(to, x).wait_send()
        home_x(to, x).wait_send()
        home_c(to, x).wait_send()

        def drain_x(j, _, to=to):
            x_copy(0, to, x, j).wait_send()
            x_copy(1, to, x, j).wait_send()
            return _

        lax.fori_loop(0, pairs, drain_x, 0)

    def drain_y(i, _):
        t = target(i)
        fan_copy(0, t, y).wait_send()
        fan_copy(1, t, y).wait_send()
        ret_copy(t, y).wait_send()
        c_copy(t, y).wait_send()
        return _

    lax.fori_loop(0, n - 1, drain_y, 0)

    def drain_twin(i, _):
        twin_copy(0, i).wait_send()
        twin_copy(1, i).wait_send()
        give_copy(i).wait_send()
        return _

    lax.fori_loop(0, n, drain_twin, 0)
    rdma(c_own, c_got, cx_ss, cx_rs, twin).wait_send()


def routed(sx, sdy, marks, wg, wu, wd, n, room):
    nz, chunk, wide = sx.shape
    lanes = nz * chunk
    hidden = wg.shape[1]
    pairs = nz // 2
    dma = pltpu.SemaphoreType.DMA
    block = (n, room, wide)
    by_x = (NX, lanes // NX, wide)
    vmem = pl.BlockSpec(memory_space=pltpu.VMEM)
    hbm = pl.BlockSpec(memory_space=pl.ANY)
    half = META // 2
    return pl.pallas_call(
        kernel,
        out_shape=(
            jax.ShapeDtypeStruct((nz, chunk, wide), BF16),
            jax.ShapeDtypeStruct((nz, 8, half), F32),
        ),
        in_specs=[vmem] * 3 + [hbm] * 3,
        out_specs=(vmem, vmem),
        scratch_shapes=[
            pltpu.VMEM(wg.shape, BF16),
            pltpu.VMEM(wu.shape, BF16),
            pltpu.VMEM(wd.shape, BF16),
            pltpu.VMEM(sx.shape, BF16),
            pltpu.VMEM(sx.shape, BF16),
            pltpu.VMEM((nz * 8, half), F32),
            pltpu.VMEM(by_x, BF16),
            pltpu.VMEM(by_x, BF16),
            pltpu.VMEM(by_x, BF16),
            pltpu.VMEM(by_x, BF16),
            pltpu.VMEM((NX * nz * 8, half), F32),
            pltpu.VMEM((n, room, lanes), BF16),
            pltpu.VMEM((lanes, wide), BF16),
            pltpu.VMEM(block, BF16),
            pltpu.VMEM(block, BF16),
            pltpu.VMEM((n, room, 2 * wide), BF16),
            pltpu.VMEM((n, room, 2 * wide), BF16),
            pltpu.VMEM((room, hidden), F32),
            pltpu.VMEM((room, hidden), F32),
            pltpu.VMEM((room, hidden), F32),
            pltpu.VMEM((room, hidden), BF16),
            pltpu.VMEM((room, hidden), BF16),
            pltpu.VMEM(block, F32),
            pltpu.VMEM(block, BF16),
            pltpu.VMEM(block, BF16),
            pltpu.VMEM(block, BF16),
            pltpu.VMEM(block, BF16),
            pltpu.VMEM((8, room), F32),
            pltpu.VMEM((8, room), F32),
            pltpu.VMEM((n, 8, room), F32),
            pltpu.VMEM((lanes, 2 * wide), F32),
            pltpu.VMEM(by_x, BF16),
            pltpu.VMEM(by_x, BF16),
            pltpu.VMEM(sx.shape, BF16),
            pltpu.VMEM((NX, 2 * nz, half), F32),
            pltpu.VMEM((NX * 2 * nz, half), F32),
            pltpu.VMEM((nz, 8, half), F32),
            pltpu.VMEM((nz, 8, half), F32),
            pltpu.VMEM(sx.shape, BF16),
            dma((3,)),
            dma((3, nz)),
            dma((3, nz)),
            dma((2, NX, pairs)),
            dma((2, NX, pairs)),
            dma((NX,)),
            dma((NX,)),
            dma((n, 2)),
            dma((n, 2)),
            dma((n, 2)),
            dma((n, 2)),
            dma((n,)),
            dma((n,)),
            dma((n,)),
            dma((n,)),
            dma,
            dma,
            dma((n,)),
            dma((n,)),
            dma((NX,)),
            dma((NX,)),
            dma((NX,)),
            dma((NX,)),
            dma((2, nz)),
            dma((2, nz)),
        ],
        compiler_params=pltpu.CompilerParams(
            collective_id=0, has_side_effects=True, vmem_limit_bytes=48 << 20
        ),
        cost_estimate=pl.CostEstimate(
            flops=10 * room * hidden * n * 2 * wide, bytes_accessed=8 << 20, transcendentals=0
        ),
    )(sx, sdy, marks, wg, wu, wd)


def shards(inputs, out_grad, expert_ids, gate_probs, group_slot, w_gate, w_up, w_down):
    n_grp = lax.axis_size("grp")
    n_loc = lax.axis_size("loc")
    exp_grp = n_loc // 2
    tok, wide = inputs.shape
    room = 2 * tok
    send = max(1, 3 * tok // 16)
    lanes = n_grp * send
    pad = META // exp_grp
    nz = n_grp // NX

    group = expert_ids // exp_grp
    member = expert_ids % exp_grp
    sent = group_slot < send
    order = group % nz * NX + group // nz
    lane = jnp.where(sent, order * send + group_slot, lanes)
    place = jnp.any(
        lane.T[None] == jnp.arange(lanes, dtype=I32)[:, None, None], axis=1
    ).astype(BF16)
    field = jnp.where(sent, member * pad + group_slot, META).reshape(-1)
    of_group = (order.reshape(-1)[None, :] == jnp.arange(n_grp, dtype=I32)[:, None]).astype(BF16)
    of_field = field[:, None] == jnp.arange(META, dtype=I32)[None, :]
    marks = dot(
        of_group, jnp.where(of_field, gate_probs.reshape(-1)[:, None], jnp.zeros((), BF16))
    )
    home_x, home_c = routed(
        dot(place, inputs).astype(BF16).reshape(nz, NX * send, wide),
        dot(place, out_grad).astype(BF16).reshape(nz, NX * send, wide),
        marks.reshape(nz, 2 * NX, META // 2),
        w_gate[0],
        w_up[0],
        w_down[0],
        exp_grp,
        room,
    )
    in_grad = lax.dot_general(
        place,
        home_x.reshape(lanes, wide),
        (((0,), (0,)), ((), ())),
        preferred_element_type=F32,
    ).astype(BF16)
    table = home_c.reshape(nz, 2, NX, META // 2).transpose(0, 2, 1, 3).reshape(n_grp, META)
    picks = lax.dot_general(
        of_group, table.astype(BF16), (((0,), (0,)), ((), ())), preferred_element_type=F32
    )
    gate_grad = jnp.sum(jnp.where(of_field, picks, 0.0), axis=1).astype(BF16)
    return in_grad, gate_grad.reshape(expert_ids.shape)


def solution(mesh):
    return jax.shard_map(
        shards,
        mesh=mesh,
        in_specs=(
            P("grp", "loc"),
            P("grp", "loc"),
            P("grp", None),
            P("grp", None),
            P("grp", None),
            P(("grp", "loc"), None, None),
            P(("grp", "loc"), None, None),
            P(("grp", "loc"), None, None),
        ),
        out_specs=(P("grp", "loc"), P("grp", None)),
        check_vma=False,
    )
```

time: 179 us -> 147 us (0.82); the launches traced: 176 us -> 147 us
  Pallas kernels: 56.1 us -> 139 us
  waiting for transfers between devices: 45.4 us -> 0 us
  blocking collectives: 37.9 us -> 0 us
  starting transfers between devices: 22.8 us -> 0 us
  local copies, waits for them, and re-layouts: 6.52 us -> 2.36 us
    pallas_call x1, Pallas kernels: 56.1 us -> 139 us  [routed(): pl.pallas_call(kernel, out_shape=(jax.ShapeDtypeStruct((nz, chunk, wide),...]
    all_to_all x1 -> x0, waiting for transfers between devices: 45.4 us -> none  [shards(): lax.all_to_all(outgoing, 'grp', split_axis=0, concat_axis=0, tiled=True)]
    all_to_all x1 -> x0, blocking collectives: 37.9 us -> none  [shards(): lax.all_to_all(jnp.concatenate([summed.reshape(n_grp, send, wide), home_c...]
    all_to_all x1 -> x0, starting transfers between devices: 22.8 us -> none  [shards(): lax.all_to_all(outgoing, 'grp', split_axis=0, concat_axis=0, tiled=True)]
  transfers between devices with their start and end apart: 1 -> 0, of which waited for: 1 -> 0; matrix products, arithmetic and copies ran while one was open for 0% -> 0% of each run, Pallas kernels for 0% -> 0%
where the time goes in v3:
time: 147 us
  Pallas kernels  139 us (95%)
  matrix products  3.05 us (2%)
  local copies, waits for them, and re-layouts  2.36 us (2%)
  other arithmetic  2.15 us (1%)
    pallas_call x1, Pallas kernels, routed(): pl.pallas_call(kernel, out_shape=(jax.ShapeDtypeStruct((nz, chunk, wide),...  139 us

profile of v3, /device:TPU:1, one launch (start us, length us, event | category | flops | bytes accessed | tf_op | source)
XLA Modules:
  0.0 147.1 jit_solution(12163876126262938395)
XLA Ops:
  0.6 0.0 copy-start
  0.6 0.0 copy-start.3
  0.7 0.8 select_bitcast_fusion
  1.5 0.8 copy.17
  2.3 0.1 broadcast_in_dim.31
  2.5 0.1 copy.15
  2.6 0.1 eq.49
  2.7 0.1 copy.16
  2.8 0.1 eq.53
  3.0 0.0 copy-start.2
  3.0 0.3 fusion.3
  3.3 0.0 copy-start.1
  3.4 1.3 fusion
  4.7 0.0 copy-done
  4.7 0.3 convolution_convert_fusion
  5.0 1.0 convolution_convert_fusion.1
  6.0 0.0 copy-done.3
  6.0 0.0 copy-done.2
  6.0 0.0 copy-done.1
  6.0 138.8 %shard_map.95 = (bf16[16,96,128]{2,1,0:T(8,128)(2,1)S(1)}, f32[16,8,128]{2,1,0:T(8,128)S(1)}) custom-call(bf16[16,96,128]{2,1,0:T(8,128)(2,1)S(1)} %bitcast.22, bf16[16,96,128]{2,1,0:T(8,128)(2,1)S(1)} %bitcast.21, f32[16,8,128]{2,1,0:T(8,128)S(1)} %reshape.29.marks_ref, bf16[2048,256]{1,0:T(8,128)(2,1)S(1)} %bitcast.23, bf16[2048,256]{1,0:T(8,128)(2,1)S(1)} %bitcast.24, ...), custom_call_target="tpu_custom_call" | custom-call | flops 1342177280 | bytes 8388608 | tf_op jit(solution)/shard_map/pallas_call | solution.py:566
  144.8 1.0 convolution_convert_fusion.2
  145.9 0.4 fusion.2
  146.3 0.2 convert_element_type.38
  146.4 0.7 copy.19
  (3 shorter events, 0.0 us)
Async XLA Ops:
  0.6 4.0 %copy-start = (bf16[128,128]{1,0:T(8,128)(2,1)S(1)}, bf16[128,128]{1,0:T(8,128)(2,1)}, u32[]{:S(2)}) copy-start(bf16[128,128]{1,0:T(8,128)(2,1)} %param.9) | copy-start | bytes 98308
  0.6 5.3 %copy-start.3 = (bf16[1,256,2048]{2,1,0:T(8,128)(2,1)S(1)}, bf16[1,256,2048]{2,1,0:T(8,128)(2,1)}, u32[]{:S(2)}) copy-start(bf16[1,256,2048]{2,1,0:T(8,128)(2,1)} %param.15) | copy-start | bytes 3145732
  3.0 3.0 %copy-start.2 = (bf16[1,2048,256]{2,1,0:T(8,128)(2,1)S(1)}, bf16[1,2048,256]{2,1,0:T(8,128)(2,1)}, u32[]{:S(2)}) copy-start(bf16[1,2048,256]{2,1,0:T(8,128)(2,1)} %param.14) | copy-start | bytes 3145732
  3.3 2.7 %copy-start.1 = (bf16[1,2048,256]{2,1,0:T(8,128)(2,1)S(1)}, bf16[1,2048,256]{2,1,0:T(8,128)(2,1)}, u32[]{:S(2)}) copy-start(bf16[1,2048,256]{2,1,0:T(8,128)(2,1)} %param.13) | copy-start | bytes 3145732

commit v4 on v3

--- a/solution.py
+++ b/solution.py
@@ -33,26 +33,27 @@
 
 
 def kernel(
-    sx_ref, sdy_ref, marks_ref, wg_hbm, wu_hbm, wd_hbm,
+    x_ref, dy_ref, marks_ref, wg_hbm, wu_hbm, wd_hbm,
     out_x, out_c,
     wg_ref, wu_ref, wd_ref,
-    z_dy, z_x, z_marks, x_dy, x_x, l_dy, l_x, l_marks, pick_ref, rank_ref,
+    raw_dy, raw_x, z_marks, place_ref, x_dy, x_x, l_dy, l_x, x_marks, l_marks, y_marks,
+    pick_ref, rank_ref, row_ref,
     fan_x, fan_dy, full_x, full_dy, acc_g, acc_u, acc_b, dg_ref, du_ref,
-    keep, give, got, pair, back, c_own, c_got, c_all, acc,
+    keep, give, got, pair, back, gate_ref, c_own, c_got, c_all, acc,
     o_x, m_x, h_x, o_c, m_c, s_c, h_c, zo_x,
-    w_sem, z_ss, z_rs, x_ss, x_rs, xm_ss, xm_rs,
+    w_sem, z_ss, z_rs, ag_ss, ag_rs, x_ss, x_rs, xm_ss, xm_rs, ym_ss, ym_rs,
     fan_ss, fan_rs, twin_ss, twin_rs, give_ss, give_rs, ret_ss, ret_rs,
     cx_ss, cx_rs, cr_ss, cr_rs, hx_ss, hx_rs, hc_ss, hc_rs, hz_ss, hz_rs,
 ):
     n = full_x.shape[0]
     room, wide = fan_x.shape[1:]
-    nz, chunk = z_x.shape[:2]
+    nz, chunk = zo_x.shape[:2]
+    tok = x_ref.shape[0]
     send = chunk // NX
     two = 2 * send
     pairs = nz // 2
     lanes = nz * chunk
     n_grp = NX * nz
-    pad = META // n
     half = META // 2
     grp = lax.axis_index("grp")
     loc = lax.axis_index("loc")
@@ -106,37 +107,98 @@
     def eight(slot):
         return pl.ds(pl.multiple_of(slot * 8, 8), 8)
 
-    def z_copy(k, to, slot):
-        src = (marks_ref, sdy_ref, sx_ref)[k].at[to]
-        dst = (z_marks.at[eight(slot)], z_dy.at[slot], z_x.at[slot])[k]
-        return rdma(src, dst, z_ss.at[k, to], z_rs.at[k, slot], at_z(to))
-
-    for k in range(3):
-
-        def z_send(i, _, k=k):
-            z_copy(k, (z + ring_offset(i, nz)) % nz, z).start()
-            return _
-
-        lax.fori_loop(0, nz - 1, z_send, 0)
-
+    def ag_copy(k, block, idx, hop):
+        raw = (raw_dy, raw_x)[k]
+        return rdma(
+            raw.at[block], raw.at[block], ag_ss.at[k, idx], ag_rs.at[k, block],
+            at_z((z + hop + nz) % nz),
+        )
+
+    def passes(k, away):
+        if away == 0:
+            return ((0, 3), (1, -3), (2, 1), (3, -1))
+        sign = 1 if away > 0 else -1
+        base = {3: 4, -3: 7, 6: 10, -6: 13}[away]
+        hops = ((base, 3 * sign), (base + 1, sign), (base + 2, -sign))
+        if abs(away) == 3:
+            return hops
+        last = ((base + 2, 2 * sign),) if k == (0 if sign > 0 else 1) else ()
+        return ((base, sign), (base + 1, -sign)) + last
+
+    def arrived(k, block):
+        ag_copy(k, block, 0, 1).wait_recv()
+
+    def pass_on(k, away):
+        block = (z - away + nz) % nz
+        if away != 0:
+            arrived(k, block)
+        for idx, hop in passes(k, away):
+            ag_copy(k, block, idx, hop).start()
+
+    def meta_copy(to, slot):
+        return rdma(
+            marks_ref.at[to], z_marks.at[eight(slot)], z_ss.at[to], z_rs.at[slot], at_z(to)
+        )
+
+    raw_dy[z] = dy_ref[...]
+    pass_on(0, 0)
+
+    def meta_send(i, _):
+        meta_copy((z + ring_offset(i, nz)) % nz, z).start()
+        return _
+
+    lax.fori_loop(0, nz - 1, meta_send, 0)
     z_marks[eight(z)] = marks_ref[z]
-    z_dy[z] = sdy_ref[z]
-    z_x[z] = sx_ref[z]
+    raw_x[z] = x_ref[...]
+    for away in (3, -3):
+        pass_on(0, away)
+    pass_on(1, 0)
+
+    def meta_in(i, _):
+        meta_copy((z + i) % nz, (z + i) % nz).wait_recv()
+        return _
+
+    lax.fori_loop(1, nz, meta_in, 0)
 
     def all_z(slot):
-        return pl.ds(pl.multiple_of(slot * nz * 8, 8), nz * 8)
+        return pl.ds(pl.multiple_of(slot * nz, 8), nz)
 
     def marks_copy(to, slot):
-        return rdma(z_marks, l_marks.at[all_z(slot)], xm_ss.at[to], xm_rs.at[slot], at_x(to))
-
-    def marks_in(i, _):
-        z_copy(0, (z + i) % nz, (z + i) % nz).wait_recv()
-        return _
-
-    lax.fori_loop(1, nz, marks_in, 0)
+        return rdma(x_marks, l_marks.at[all_z(slot)], xm_ss.at[to], xm_rs.at[slot], at_x(to))
+
+    x_marks[...] = z_marks[pl.ds(NX, nz, 8), :]
+    l_marks[all_z(x)] = x_marks[...]
     for dx in range(1, NX):
         marks_copy((x + dx) % NX, x).start()
-    l_marks[all_z(x)] = z_marks[...]
+    for k, away in ((0, 6), (0, -6), (1, 3), (1, -3)):
+        pass_on(k, away)
+    slot_rows = lax.broadcasted_iota(I32, (send, half), 0).astype(F32)
+
+    def place(i, _):
+        parts = [z_marks[pl.ds(i * 8 + xx, 1), :] == slot_rows for xx in range(NX)]
+        place_ref[i] = bits(jnp.concatenate([part.astype(F32) for part in parts], axis=0) > 0.5)
+        return _
+
+    lax.fori_loop(0, nz, place, 0)
+    for dx in range(1, NX):
+        marks_copy((x + dx) % NX, (x + dx) % NX).wait_recv()
+    pad = META // n
+    per = half // pad
+    part = half // NX
+    take_row = lax.broadcasted_iota(I32, (half, half), 0)
+    take_col = lax.broadcasted_iota(I32, (half, half), 1)
+    inside = (take_row >= x * part) & (take_row < x * part + part)
+    take = bits(inside & (take_row - x * part == take_col - (y % per) * pad))
+    y_marks[y] = dot(l_marks[...].astype(BF16), take).astype(BF16)
+
+    def gates_copy(to, slot):
+        return rdma(y_marks.at[y], y_marks.at[slot], ym_ss.at[to], ym_rs.at[slot], peer(to))
+
+    def gates_send(i, _):
+        gates_copy((y + ring_offset(i, n)) % n, y).start()
+        return _
+
+    lax.fori_loop(0, n - 1, gates_send, 0)
 
     def pair_rows(j):
         return pl.ds(pl.multiple_of(j * two, 16 if two % 16 == 0 else 1), two)
@@ -149,21 +211,24 @@
         )
 
     def onward(k, i):
-        src, out, land = ((z_dy, x_dy, l_dy), (z_x, x_x, l_x))[k]
+        raw, out, land = ((raw_dy, x_dy, l_dy), (raw_x, x_x, l_x))[k]
         j = (z // 2 + near_offset(i, pairs)) % pairs
+        chosen = []
         for zz in range(2):
             slot = 2 * j + zz
-
-            @pl.when(slot != z)
+            away = (z - slot + nz) % nz
+            passed = (away == 0) | (away == 3) | (away == 6) | (away == nz - 3) | (away == nz - 6)
+
+            @pl.when(jnp.logical_not(passed))
             def _arrival():
-                z_copy(1 + k, slot, slot).wait_recv()
-
-        even = src[2 * j].astype(F32)
-        odd = src[2 * j + 1].astype(F32)
+                arrived(k, slot)
+
+            chosen.append(dot(place_ref[slot][:, :tok], raw[slot]))
+        even, odd = chosen
         rows = pair_rows(j)
         for xx in range(NX):
-            part = slice(xx * send, (xx + 1) * send)
-            both = jnp.concatenate([even[part], odd[part]], axis=0).astype(BF16)
+            mine = slice(xx * send, (xx + 1) * send)
+            both = jnp.concatenate([even[mine], odd[mine]], axis=0).astype(BF16)
 
             @pl.when(xx != x)
             def _far():
@@ -174,14 +239,12 @@
             def _near():
                 land[xx, rows] = both
 
-    def onward_dy(i, _):
-        onward(0, i)
-        return _
-
-    lax.fori_loop(0, pairs, onward_dy, 0)
-
-    for dx in range(1, NX):
-        marks_copy((x + dx) % NX, (x + dx) % NX).wait_recv()
+    def gates_in(i, _):
+        slot = (y + i) % n
+        gates_copy(slot, slot).wait_recv()
+        return _
+
+    lax.fori_loop(1, n, gates_in, 0)
     f_row = lax.broadcasted_iota(I32, (half, half), 0)
     f_col = lax.broadcasted_iota(I32, (half, half), 1)
     same = f_row // pad == f_col // pad
@@ -198,9 +261,10 @@
     slot_of = (col_f % pad) == (lane_f % send)
     rank_cols = jnp.zeros((lanes, wide), F32)
     gate_cols = jnp.zeros((lanes, wide), F32)
-    per = half // pad
     for ab in range(2):
-        marks = l_marks[pl.ds(2 * x + ab, n_grp, 8), :]
+        marks = y_marks[ab * per].astype(F32)
+        for m in range(1, per):
+            marks = marks + y_marks[ab * per + m].astype(F32)
         picked = marks != 0.0
         count = bits(picked)
         within = dot(count, upto)
@@ -214,16 +278,17 @@
         gates = jnp.where(slot_of, dot(from_src, marks.astype(BF16)), 0.0).astype(BF16)
         rank_cols = rank_cols + dot(ranks, fold)
         gate_cols = gate_cols + dot(gates, fold)
+    for away in (6, -6):
+        pass_on(1, away)
+    def onward_dy(i, _):
+        onward(0, i)
+        return _
+
+    lax.fori_loop(0, pairs, onward_dy, 0)
     rank_ref[...] = rank_cols.astype(BF16)
     gate_cols = gate_cols.astype(BF16)
-    rank_rows = rank_cols.T[:8]
+    row_ref[...] = rank_cols.T[:8]
     slot_iota = lax.broadcasted_iota(I32, (room, lanes), 0).astype(F32)
-    for m in range(n):
-        pick_ref[m] = bits(rank_rows[m : m + 1, :] == slot_iota)
-    gate_slots = dot(pick_ref[y], gate_cols)
-    my_lane = lax.broadcasted_iota(I32, (room, wide), 1) == y
-    gate_col = jnp.sum(jnp.where(my_lane, gate_slots, 0.0), axis=1, keepdims=True)
-
     def fan_copy(k, m, slot):
         src, dst = ((fan_dy, full_dy), (fan_x, full_x))[k]
         return rdma(
@@ -261,6 +326,8 @@
 
         def one(i, _):
             m = (y + ring_offset(i, n)) % n
+            if k == 0:
+                pick_ref[m] = bits(row_ref[pl.ds(m, 1), :] == slot_iota)
             out = dot(pick_ref[m], rows).astype(BF16)
 
             @pl.when(i < n - 1)
@@ -289,6 +356,9 @@
         return pl.ds(pl.multiple_of(slot * 2 * wide, 2 * wide), 2 * wide)
 
     spread(0)
+    gate_slots = dot(pick_ref[y], gate_cols)
+    my_lane = lax.broadcasted_iota(I32, (room, wide), 1) == y
+    gate_col = jnp.sum(jnp.where(my_lane, gate_slots, 0.0), axis=1, keepdims=True)
     acc_g[...] = jnp.zeros_like(acc_g)
     acc_u[...] = jnp.zeros_like(acc_u)
     acc_b[...] = jnp.zeros_like(acc_b)
@@ -342,24 +412,13 @@
     q = gate_col * b
     dg_ref[...] = (q * u * (s * (1.0 + g * (1.0 - s)))).astype(BF16)
     du_ref[...] = (q * a).astype(BF16)
-    gate_part = a * u * b
-    high = gate_part.astype(BF16)
-    low = (gate_part - high.astype(F32)).astype(BF16)
-    ones = jnp.ones((8, gate_part.shape[1]), BF16)
-    c_half = lax.dot_general(ones, high, NT, preferred_element_type=F32) + lax.dot_general(
-        ones, low, NT, preferred_element_type=F32
-    )
-    c_own[...] = c_half.astype(BF16).astype(F32)
-    rdma(c_own, c_got, cx_ss, cx_rs, twin).start()
+    gate_ref[...] = a * u * b
 
     def give_copy(t):
         return rdma(give.at[t], got.at[t], give_ss.at[t], give_rs.at[t], twin)
 
     def ret_copy(t, slot):
         return rdma(pair.at[t], back.at[slot], ret_ss.at[t], ret_rs.at[slot], peer(t))
-
-    def c_copy(t, slot):
-        return rdma(c_all.at[y], c_all.at[slot], cr_ss.at[t], cr_rs.at[slot], peer(t))
 
     def target(i):
         return (y + ring_offset(i, n)) % n
@@ -395,104 +454,114 @@
         return _
 
     lax.fori_loop(0, n, produce, 0)
-    rdma(c_own, c_got, cx_ss, cx_rs, twin).wait_recv()
-    c_all[y] = (c_own[...] + c_got[...]).astype(BF16).astype(F32)
-
-    def c_send(i, _):
-        c_copy(target(i), y).start()
-        return _
-
-    lax.fori_loop(0, n - 1, c_send, 0)
-
     add_pair(n - 1)
+    gate_part = gate_ref[...]
+    high = gate_part.astype(BF16)
+    low = (gate_part - high.astype(F32)).astype(BF16)
+    ones = jnp.ones((8, gate_part.shape[1]), BF16)
+    c_half = lax.dot_general(ones, high, NT, preferred_element_type=F32) + lax.dot_general(
+        ones, low, NT, preferred_element_type=F32
+    )
+    c_own[...] = c_half.astype(BF16).astype(F32)
+    rdma(c_own, c_got, cx_ss, cx_rs, twin).start()
 
     acc[...] = jnp.zeros_like(acc)
     lane_iota = lax.broadcasted_iota(I32, (lanes, room), 1).astype(F32)
-    eye = lax.broadcasted_iota(I32, (room, room), 0) == lax.broadcasted_iota(I32, (room, room), 1)
-    col_iota = lax.broadcasted_iota(I32, (room, wide), 1)
     pick_row = lax.broadcasted_iota(I32, (wide, room), 0)
 
     def combine(slot):
         rank = dot(rank_ref[...], bits(pick_row == slot))
         pick = bits(rank == lane_iota)
-        c_col = jnp.sum(jnp.where(eye, c_all[slot][:1, :], 0.0), axis=1, keepdims=True)
-        c_cols = jnp.where(col_iota == slot, c_col, 0.0).astype(BF16)
-        acc[...] += dot(pick, jnp.concatenate([back[slot], c_cols], axis=1))
+        acc[...] += dot(pick, back[slot])
 
     combine(y)
+
+    rdma(c_own, c_got, cx_ss, cx_rs, twin).wait_recv()
+    c_lane = dot((c_own[...] + c_got[...]).astype(BF16), pick_ref[y])[:1, :]
+    lane_to = lax.broadcasted_iota(I32, (n_grp, lanes), 1)
+    src_to = lax.broadcasted_iota(I32, (n_grp, lanes), 0) * send
+    c_rows = jnp.where((lane_to >= src_to) & (lane_to < src_to + send), c_lane, 0.0)
+    c_spot = bits(col_f - x * part == lane_f % send)
+    table = dot(c_rows.astype(BF16), c_spot)
+    for xx in range(NX):
+        o_c[xx] = table[xx * nz : (xx + 1) * nz]
+
+    def home_c(to, slot):
+        return rdma(o_c.at[to], m_c.at[slot], hc_ss.at[to], hc_rs.at[slot], at_x(to))
+
+    for dx in range(1, NX):
+        home_c((x + dx) % NX, x).start()
 
     def collect(i, _):
         slot = source(i)
         ret_copy(slot, slot).wait_recv()
-        c_copy(slot, slot).wait_recv()
         combine(slot)
         return _
 
     lax.fori_loop(0, n - 1, collect, 0)
 
-    total = acc[:, :wide].astype(BF16).reshape(NX, nz * send, wide)
-    lane_c = acc[:, wide:].astype(BF16)
-    un_row = lax.broadcasted_iota(I32, (wide, half), 0)
-    un_col = lax.broadcasted_iota(I32, (wide, half), 1)
-    lane_to = lax.broadcasted_iota(I32, (n_grp, lanes), 1)
-    src_to = lax.broadcasted_iota(I32, (n_grp, lanes), 0) * send
-    to_src = bits((lane_to >= src_to) & (lane_to < src_to + send))
-
-    def home_x(to, slot):
-        return rdma(o_x.at[to], m_x.at[slot], hx_ss.at[to], hx_rs.at[slot], at_x(to))
-
-    def both_z(slot):
-        return pl.ds(pl.multiple_of(slot * 2 * nz, 8), 2 * nz)
-
-    def home_c(to, slot):
-        return rdma(o_c.at[to], m_c.at[both_z(slot)], hc_ss.at[to], hc_rs.at[slot], at_x(to))
+    total = acc[...].astype(BF16).reshape(NX, nz * send, wide)
+    def home_x(to, slot, j):
+        rows = pair_rows(j)
+        return rdma(
+            o_x.at[to, rows], m_x.at[slot, rows], hx_ss.at[to, j], hx_rs.at[slot, j], at_x(to)
+        )
 
     for xx in range(NX):
 
         @pl.when(xx != x)
         def _far():
             o_x[xx] = total[xx]
-            home_x(xx, x).start()
 
         @pl.when(xx == x)
         def _near():
             m_x[xx] = total[xx]
 
-    for ab in range(2):
-        spread_c = dot(lane_c, bits(un_col // pad + ab * per == un_row))
-        table = dot(to_src, jnp.where(slot_of, spread_c, 0.0).astype(BF16))
-        for xx in range(NX):
-            o_c[xx, ab * nz : (ab + 1) * nz, :] = table[xx * nz : (xx + 1) * nz]
-    for dx in range(1, NX):
-        home_c((x + dx) % NX, x).start()
-    m_c[both_z(x)] = o_c[x]
-    for dx in range(1, NX):
-        xx = (x + dx) % NX
-        home_x(xx, xx).wait_recv()
-        home_c(xx, xx).wait_recv()
+    def home_order(i):
+        return (z // 2 + ring_offset(i, pairs)) % pairs
+
+    def home_send(i, _):
+        for dx in range(1, NX):
+            home_x((x + dx) % NX, x, home_order(i)).start()
+        return _
+
+    lax.fori_loop(0, pairs, home_send, 0)
 
     def home_z(k, to, slot):
         src, dst = ((zo_x, h_x), (s_c, h_c))[k]
         return rdma(src.at[to], dst.at[slot], hz_ss.at[k, to], hz_rs.at[k, slot], at_z(to))
 
+    for dx in range(1, NX):
+        xx = (x + dx) % NX
+        home_c(xx, xx).wait_recv()
+    merged = o_c[x]
+    for dx in range(1, NX):
+        merged = merged + m_c[(x + dx) % NX]
+    for zz in range(nz):
+        s_c[zz] = merged[zz : zz + 1]
+
+    def off_c(i, _):
+        home_z(1, (z + ring_offset(i, nz)) % nz, z).start()
+        return _
+
+    lax.fori_loop(0, nz - 1, off_c, 0)
+
     def off(i, _):
-        j = (z // 2 + ring_offset(i, pairs)) % pairs
+        j = home_order(i)
         rows = pair_rows(j)
+        for dx in range(1, NX):
+            xx = (x + dx) % NX
+            home_x(xx, xx, j).wait_recv()
         parts = [m_x[xx, rows].astype(F32) for xx in range(NX)]
         for zz in range(2):
             to = 2 * j + zz
             zo_x[to] = jnp.concatenate(
                 [part[zz * send : (zz + 1) * send] for part in parts], axis=0
             ).astype(BF16)
-            for ab in range(2):
-                s_c[to, ab * NX : (ab + 1) * NX, :] = m_c[
-                    pl.ds(ab * nz + to, NX, 2 * nz), :
-                ]
 
             @pl.when(to != z)
             def _far():
                 home_z(0, to, z).start()
-                home_z(1, to, z).start()
 
         return _
 
@@ -500,20 +569,39 @@
     h_x[z] = zo_x[z]
     h_c[z] = s_c[z]
 
-    def home_in(i, _):
-        slot = (z + i) % nz
-        home_z(0, slot, slot).wait_recv()
-        home_z(1, slot, slot).wait_recv()
-        return _
-
-    lax.fori_loop(1, nz, home_in, 0)
+    def home_in(k):
+        def one(i, _):
+            slot = (z + i) % nz
+            home_z(k, slot, slot).wait_recv()
+            return _
+
+        lax.fori_loop(1, nz, one, 0)
+
+    home_in(1)
+    for zz in range(nz):
+        c_all[y, zz : zz + 1, :] = h_c[zz]
+
+    def c_copy(t, slot):
+        return rdma(c_all.at[y], c_all.at[slot], cr_ss.at[t], cr_rs.at[slot], peer(t))
+
+    def c_send(i, _):
+        c_copy(target(i), y).start()
+        return _
+
+    lax.fori_loop(0, n - 1, c_send, 0)
+    home_in(0)
+
+    def c_in(i, _):
+        c_copy(source(i), source(i)).wait_recv()
+        return _
+
+    lax.fori_loop(0, n - 1, c_in, 0)
     out_x[...] = h_x[...]
-    out_c[...] = h_c[...]
+    out_c[...] = c_all[...]
 
     def drain_z(i, _):
         to = (z + i) % nz
-        for k in range(3):
-            z_copy(k, to, z).wait_send()
+        meta_copy(to, z).wait_send()
         home_z(0, to, z).wait_send()
         home_z(1, to, z).wait_send()
         return _
@@ -522,18 +610,24 @@
     for dx in range(1, NX):
         to = (x + dx) % NX
         marks_copy(to, x).wait_send()
-        home_x(to, x).wait_send()
         home_c(to, x).wait_send()
 
         def drain_x(j, _, to=to):
             x_copy(0, to, x, j).wait_send()
             x_copy(1, to, x, j).wait_send()
+            home_x(to, x, j).wait_send()
             return _
 
         lax.fori_loop(0, pairs, drain_x, 0)
+
+    for k in range(2):
+        for away in (0, 3, -3, 6, -6):
+            for idx, hop in passes(k, away):
+                ag_copy(k, z, idx, hop).wait_send()
 
     def drain_y(i, _):
         t = target(i)
+        gates_copy(t, y).wait_send()
         fan_copy(0, t, y).wait_send()
         fan_copy(1, t, y).wait_send()
         ret_copy(t, y).wait_send()
@@ -552,9 +646,13 @@
     rdma(c_own, c_got, cx_ss, cx_rs, twin).wait_send()
 
 
-def routed(sx, sdy, marks, wg, wu, wd, n, room):
-    nz, chunk, wide = sx.shape
+def routed(x, dy, marks, wg, wu, wd, n, room, send):
+    nz = marks.shape[0]
+    tok, wide = x.shape
+    chunk = NX * send
     lanes = nz * chunk
+    tokens = (nz, tok, wide)
+    packed = (nz, chunk, wide)
     hidden = wg.shape[1]
     pairs = nz // 2
     dma = pltpu.SemaphoreType.DMA
@@ -566,8 +664,8 @@
     return pl.pallas_call(
         kernel,
         out_shape=(
-            jax.ShapeDtypeStruct((nz, chunk, wide), BF16),
-            jax.ShapeDtypeStruct((nz, 8, half), F32),
+            jax.ShapeDtypeStruct(packed, BF16),
+            jax.ShapeDtypeStruct((n, nz, half), F32),
         ),
         in_specs=[vmem] * 3 + [hbm] * 3,
         out_specs=(vmem, vmem),
@@ -575,16 +673,20 @@
             pltpu.VMEM(wg.shape, BF16),
             pltpu.VMEM(wu.shape, BF16),
             pltpu.VMEM(wd.shape, BF16),
-            pltpu.VMEM(sx.shape, BF16),
-            pltpu.VMEM(sx.shape, BF16),
+            pltpu.VMEM(tokens, BF16),
+            pltpu.VMEM(tokens, BF16),
             pltpu.VMEM((nz * 8, half), F32),
+            pltpu.VMEM((nz, chunk, half), BF16),
             pltpu.VMEM(by_x, BF16),
             pltpu.VMEM(by_x, BF16),
             pltpu.VMEM(by_x, BF16),
             pltpu.VMEM(by_x, BF16),
-            pltpu.VMEM((NX * nz * 8, half), F32),
+            pltpu.VMEM((nz, half), F32),
+            pltpu.VMEM((NX * nz, half), F32),
+            pltpu.VMEM((n, NX * nz, half), BF16),
             pltpu.VMEM((n, room, lanes), BF16),
             pltpu.VMEM((lanes, wide), BF16),
+            pltpu.VMEM((8, lanes), F32),
             pltpu.VMEM(block, BF16),
             pltpu.VMEM(block, BF16),
             pltpu.VMEM((n, room, 2 * wide), BF16),
@@ -599,25 +701,30 @@
             pltpu.VMEM(block, BF16),
             pltpu.VMEM(block, BF16),
             pltpu.VMEM(block, BF16),
+            pltpu.VMEM((room, hidden), F32),
             pltpu.VMEM((8, room), F32),
             pltpu.VMEM((8, room), F32),
-            pltpu.VMEM((n, 8, room), F32),
-            pltpu.VMEM((lanes, 2 * wide), F32),
+            pltpu.VMEM((n, nz, half), F32),
+            pltpu.VMEM((lanes, wide), F32),
             pltpu.VMEM(by_x, BF16),
             pltpu.VMEM(by_x, BF16),
-            pltpu.VMEM(sx.shape, BF16),
-            pltpu.VMEM((NX, 2 * nz, half), F32),
-            pltpu.VMEM((NX * 2 * nz, half), F32),
-            pltpu.VMEM((nz, 8, half), F32),
-            pltpu.VMEM((nz, 8, half), F32),
-            pltpu.VMEM(sx.shape, BF16),
+            pltpu.VMEM(packed, BF16),
+            pltpu.VMEM((NX, nz, half), F32),
+            pltpu.VMEM((NX, nz, half), F32),
+            pltpu.VMEM((nz, 1, half), F32),
+            pltpu.VMEM((nz, 1, half), F32),
+            pltpu.VMEM(packed, BF16),
             dma((3,)),
-            dma((3, nz)),
-            dma((3, nz)),
+            dma((nz,)),
+            dma((nz,)),
+            dma((2, 16)),
+            dma((2, nz)),
             dma((2, NX, pairs)),
             dma((2, NX, pairs)),
             dma((NX,)),
             dma((NX,)),
+            dma((n,)),
+            dma((n,)),
             dma((n, 2)),
             dma((n, 2)),
             dma((n, 2)),
@@ -630,8 +737,8 @@
             dma,
             dma((n,)),
             dma((n,)),
-            dma((NX,)),
-            dma((NX,)),
+            dma((NX, pairs)),
+            dma((NX, pairs)),
             dma((NX,)),
             dma((NX,)),
             dma((2, nz)),
@@ -643,7 +750,7 @@
         cost_estimate=pl.CostEstimate(
             flops=10 * room * hidden * n * 2 * wide, bytes_accessed=8 << 20, transcendentals=0
         ),
-    )(sx, sdy, marks, wg, wu, wd)
+    )(x, dy, marks, wg, wu, wd)
 
 
 def shards(inputs, out_grad, expert_ids, gate_probs, group_slot, w_gate, w_up, w_down):
@@ -654,8 +761,8 @@
     room = 2 * tok
     send = max(1, 3 * tok // 16)
     lanes = n_grp * send
-    pad = META // exp_grp
     nz = n_grp // NX
+    part = META // 2 // NX
 
     group = expert_ids // exp_grp
     member = expert_ids % exp_grp
@@ -665,21 +772,33 @@
     place = jnp.any(
         lane.T[None] == jnp.arange(lanes, dtype=I32)[:, None, None], axis=1
     ).astype(BF16)
-    field = jnp.where(sent, member * pad + group_slot, META).reshape(-1)
+    field = jnp.where(sent, member * part + group_slot, exp_grp * part).reshape(-1)
     of_group = (order.reshape(-1)[None, :] == jnp.arange(n_grp, dtype=I32)[:, None]).astype(BF16)
-    of_field = field[:, None] == jnp.arange(META, dtype=I32)[None, :]
+    of_field = field[:, None] == jnp.arange(exp_grp * part, dtype=I32)[None, :]
+    here = sent & (member == lax.axis_index("loc") // 2)
+    own = jnp.where(here, group_slot, META).reshape(-1)[:, None]
+    own = own == jnp.arange(part, dtype=I32)[None, :]
     marks = dot(
-        of_group, jnp.where(of_field, gate_probs.reshape(-1)[:, None], jnp.zeros((), BF16))
+        of_group, jnp.where(own, gate_probs.reshape(-1)[:, None], jnp.zeros((), BF16))
+    ).reshape(nz, 1, META // 2)
+    spots = jnp.where(
+        (order.T[None] == jnp.arange(n_grp, dtype=I32)[:, None, None]) & sent.T[None],
+        group_slot.T[None],
+        META,
     )
+    spots = jnp.min(spots, axis=1).astype(F32).reshape(nz, NX, tok)
+    spots = jnp.pad(spots, ((0, 0), (0, 0), (0, META // 2 - tok)), constant_values=META)
+    meta = jnp.concatenate([spots, marks, jnp.zeros((nz, 7 - NX, META // 2), F32)], axis=1)
     home_x, home_c = routed(
-        dot(place, inputs).astype(BF16).reshape(nz, NX * send, wide),
-        dot(place, out_grad).astype(BF16).reshape(nz, NX * send, wide),
-        marks.reshape(nz, 2 * NX, META // 2),
+        inputs,
+        out_grad,
+        meta,
         w_gate[0],
         w_up[0],
         w_down[0],
         exp_grp,
         room,
+        send,
     )
     in_grad = lax.dot_general(
         place,
@@ -687,7 +806,7 @@
         (((0,), (0,)), ((), ())),
         preferred_element_type=F32,
     ).astype(BF16)
-    table = home_c.reshape(nz, 2, NX, META // 2).transpose(0, 2, 1, 3).reshape(n_grp, META)
+    table = home_c.reshape(exp_grp, nz, NX, part).transpose(1, 2, 0, 3).reshape(n_grp, -1)
     picks = lax.dot_general(
         of_group, table.astype(BF16), (((0,), (0,)), ((), ())), preferred_element_type=F32
     )

time: 147 us -> 136 us (0.925)
  Pallas kernels: 139 us -> 125 us
  local copies, waits for them, and re-layouts: 2.36 us -> 5.48 us
    pallas_call x1, Pallas kernels: 139 us -> 125 us  [routed(): pl.pallas_call(kernel, out_shape=(jax.ShapeDtypeStruct(packed, BF16), jax...]
    unnamed x10 -> x14, local copies, waits for them, and re-layouts: 1.53 us -> 3.96 us
where the time goes in v4:
time: 136 us; the launch traced here: 135 us
  Pallas kernels  125 us (92%)
  local copies, waits for them, and re-layouts  5.48 us (4%)
  other arithmetic  2.33 us (2%)
  matrix products  1.96 us (1%)
    pallas_call x1, Pallas kernels, routed(): pl.pallas_call(kernel, out_shape=(jax.ShapeDtypeStruct(packed, BF16), jax...  125 us
    unnamed x14, local copies, waits for them, and re-layouts  3.96 us

profile of v4, /device:TPU:1, one launch (start us, length us, event | category | flops | bytes accessed | tf_op | source)
XLA Modules:
  0.0 135.5 jit_solution(11733395302113124621)
XLA Ops:
  0.6 0.0 copy-start.5
  0.6 0.0 copy-start
  0.7 0.0 copy-start.3
  0.7 0.8 select_bitcast_fusion
  1.5 0.1 copy.19
  1.6 0.1 eq.86
  1.8 0.1 copy.20
  1.9 0.1 eq.92
  2.0 0.8 copy.21
  2.8 0.1 broadcast_in_dim.54
  3.0 0.5 fusion.3
  3.5 0.1 reshape.28
  3.6 0.0 copy-done.5
  3.6 0.1 select_reduce_fusion
  3.7 0.1 pad.2.clone
  3.8 0.1 maximum_maximum_fusion.marks_ref
  3.9 0.0 copy-done
  3.9 0.0 copy-done.4
  3.9 0.0 copy-start.1
  3.9 1.2 copy-done.1
  5.1 1.2 copy-done.2
  6.3 124.9 %shard_map.95 = (bf16[16,96,128]{2,1,0:T(8,128)(2,1)S(1)}, f32[8,16,128]{2,1,0:T(8,128)S(1)}) custom-call(bf16[128,128]{1,0:T(8,128)(2,1)S(1)} %copy-done.3, bf16[128,128]{1,0:T(8,128)(2,1)S(1)} %copy-done.4, f32[16,8,128]{2,1,0:T(8,128)S(1)} %maximum_maximum_fusion.marks_ref, bf16[2048,256]{1,0:T(8,128)(2,1)S(1)} %bitcast.20, ...), custom_call_target="tpu_custom_call" | custom-call | flops 1342177280 | bytes 8388608 | tf_op jit(solution)/shard_map/pallas_call | solution.py:664
  131.3 0.1 convert_element_type.35
  131.4 0.1 copy.29
  131.5 0.1 convert_element_type.37
  131.6 0.1 copy.24
  131.8 0.1 eq.96
  131.9 0.4 fusion.1
  132.3 0.2 convert_element_type.39
  132.5 0.7 copy.26
  133.2 1.3 fusion
  134.5 1.0 convolution_convert_fusion
  (7 shorter events, 0.0 us)
Async XLA Ops:
  0.6 3.0 %copy-start.5 = (s32[128,10]{0,1:T(8,128)S(1)}, s32[128,10]{0,1:T(8,128)}, u32[]{:S(2)}) copy-start(s32[128,10]{0,1:T(8,128)} %param.12) | copy-start | bytes 15364
  0.6 3.2 %copy-start = (bf16[1,2048,256]{2,1,0:T(8,128)(2,1)S(1)}, bf16[1,2048,256]{2,1,0:T(8,128)(2,1)}, u32[]{:S(2)}) copy-start(bf16[1,2048,256]{2,1,0:T(8,128)(2,1)} %param.13) | copy-start | bytes 3145732
  0.7 3.2 %copy-start.3 = (bf16[128,128]{1,0:T(8,128)(2,1)S(1)}, bf16[128,128]{1,0:T(8,128)(2,1)}, u32[]{:S(2)}) copy-start(bf16[128,128]{1,0:T(8,128)(2,1)} %x_ref.1) | copy-start | bytes 98308
  0.7 3.2 %copy-start.4 = (bf16[128,128]{1,0:T(8,128)(2,1)S(1)}, bf16[128,128]{1,0:T(8,128)(2,1)}, u32[]{:S(2)}) copy-start(bf16[128,128]{1,0:T(8,128)(2,1)} %dy_ref.1) | copy-start | bytes 98308
  3.9 1.2 copy-start.1
  5.1 1.2 copy-start.2

commit v5 on v4

--- a/solution.py
+++ b/solution.py
@@ -238,6 +238,15 @@
             @pl.when(xx == x)
             def _near():
                 land[xx, rows] = both
+
+    for away in (6, -6):
+        pass_on(1, away)
+
+    def onward_dy(i, _):
+        onward(0, i)
+        return _
+
+    lax.fori_loop(0, pairs, onward_dy, 0)
 
     def gates_in(i, _):
         slot = (y + i) % n
@@ -278,17 +287,17 @@
         gates = jnp.where(slot_of, dot(from_src, marks.astype(BF16)), 0.0).astype(BF16)
         rank_cols = rank_cols + dot(ranks, fold)
         gate_cols = gate_cols + dot(gates, fold)
-    for away in (6, -6):
-        pass_on(1, away)
-    def onward_dy(i, _):
-        onward(0, i)
-        return _
-
-    lax.fori_loop(0, pairs, onward_dy, 0)
     rank_ref[...] = rank_cols.astype(BF16)
     gate_cols = gate_cols.astype(BF16)
     row_ref[...] = rank_cols.T[:8]
-    slot_iota = lax.broadcasted_iota(I32, (room, lanes), 0).astype(F32)
+    slot_iota = lax.broadcasted_iota(I32, (room, lanes), 0).astype(F32).astype(BF16)
+
+    def picks(m, _):
+        row = row_ref[pl.ds(m, 1), :].astype(BF16)
+        pick_ref[m] = jnp.where(row == slot_iota, jnp.ones((), BF16), jnp.zeros((), BF16))
+        return _
+
+    lax.fori_loop(0, n, picks, 0)
     def fan_copy(k, m, slot):
         src, dst = ((fan_dy, full_dy), (fan_x, full_x))[k]
         return rdma(
@@ -326,8 +335,6 @@
 
         def one(i, _):
             m = (y + ring_offset(i, n)) % n
-            if k == 0:
-                pick_ref[m] = bits(row_ref[pl.ds(m, 1), :] == slot_iota)
             out = dot(pick_ref[m], rows).astype(BF16)
 
             @pl.when(i < n - 1)
@@ -365,18 +372,17 @@
 
     def onward_x(i, _):
         onward(1, i)
-
-        @pl.when(i < n - 1)
-        def _dy():
-            hand_over(0, jnp.minimum(i, n - 2))
-
         return _
 
     lax.fori_loop(0, pairs, onward_x, 0)
-    for i in range(pairs, n - 1):
-        hand_over(0, i)
     spread(1)
     loads[2].wait()
+
+    def hand_dy(i, _):
+        hand_over(0, i)
+        return _
+
+    lax.fori_loop(0, n - 1, hand_dy, 0)
 
     def back_rows(slot, _):
         twin_arrival(0, slot).wait_recv()

time: 136 us -> 130 us (0.956)
  Pallas kernels: 125 us -> 119 us
    pallas_call x1, Pallas kernels: 125 us -> 119 us  [routed(): pl.pallas_call(kernel, out_shape=(jax.ShapeDtypeStruct(packed, BF16), jax...]
where the time goes in v5:
time: 130 us; the launch traced here: 129 us
  Pallas kernels  119 us (92%)
  local copies, waits for them, and re-layouts  5.48 us (4%)
  other arithmetic  2.33 us (2%)
  matrix products  1.96 us (2%)
    pallas_call x1, Pallas kernels, routed(): pl.pallas_call(kernel, out_shape=(jax.ShapeDtypeStruct(packed, BF16), jax...  119 us
    unnamed x14, local copies, waits for them, and re-layouts  3.96 us

profile of v5, /device:TPU:1, one launch (start us, length us, event | category | flops | bytes accessed | tf_op | source)
XLA Modules:
  0.0 129.4 jit_solution(323033424317528366)
XLA Ops:
  0.6 0.0 copy-start.5
  0.6 0.0 copy-start
  0.7 0.0 copy-start.3
  0.7 0.0 copy-start.4
  0.7 0.8 select_bitcast_fusion
  1.5 0.1 copy.19
  1.6 0.1 eq.86
  1.8 0.1 copy.20
  1.9 0.1 eq.92
  2.0 0.8 copy.21
  2.8 0.1 broadcast_in_dim.54
  3.0 0.5 fusion.3
  3.5 0.1 reshape.28
  3.6 0.0 copy-done.5
  3.6 0.1 select_reduce_fusion
  3.7 0.1 pad.2.clone
  3.8 0.1 maximum_maximum_fusion.marks_ref
  3.9 0.0 copy-done
  3.9 0.0 copy-start.1
  3.9 1.2 copy-done.1
  5.1 1.2 copy-done.2
  6.3 118.9 %shard_map.95 = (bf16[16,96,128]{2,1,0:T(8,128)(2,1)S(1)}, f32[8,16,128]{2,1,0:T(8,128)S(1)}) custom-call(bf16[128,128]{1,0:T(8,128)(2,1)S(1)} %copy-done.3, bf16[128,128]{1,0:T(8,128)(2,1)S(1)} %copy-done.4, f32[16,8,128]{2,1,0:T(8,128)S(1)} %maximum_maximum_fusion.marks_ref, bf16[2048,256]{1,0:T(8,128)(2,1)S(1)} %bitcast.20, ...), custom_call_target="tpu_custom_call" | custom-call | flops 1342177280 | bytes 8388608 | tf_op jit(solution)/shard_map/pallas_call | solution.py:670
  125.2 0.1 convert_element_type.35
  125.3 0.1 copy.29
  125.4 0.1 convert_element_type.37
  125.6 0.1 copy.24
  125.7 0.1 eq.96
  125.8 0.4 fusion.1
  126.2 0.2 convert_element_type.39
  126.4 0.7 copy.26
  127.1 1.3 %fusion = pred[1536,128]{1,0:T(8,128)(4,1)S(1)} fusion(s32[10,128]{1,0:T(8,128)S(1)} %get-tuple-element.10), kind=kLoop, calls=%fused_computation.1 | loop fusion | flops 3735552 | bytes 201728 | tf_op jit(solution)/shard_map/reduce_or | solution.py:778
  128.4 1.0 convolution_convert_fusion
  (7 shorter events, 0.0 us)
Async XLA Ops:
  0.6 3.0 %copy-start.5 = (s32[128,10]{0,1:T(8,128)S(1)}, s32[128,10]{0,1:T(8,128)}, u32[]{:S(2)}) copy-start(s32[128,10]{0,1:T(8,128)} %param.12) | copy-start | bytes 15364
  0.6 3.2 %copy-start = (bf16[1,2048,256]{2,1,0:T(8,128)(2,1)S(1)}, bf16[1,2048,256]{2,1,0:T(8,128)(2,1)}, u32[]{:S(2)}) copy-start(bf16[1,2048,256]{2,1,0:T(8,128)(2,1)} %param.13) | copy-start | bytes 3145732
  0.7 3.2 %copy-start.3 = (bf16[128,128]{1,0:T(8,128)(2,1)S(1)}, bf16[128,128]{1,0:T(8,128)(2,1)}, u32[]{:S(2)}) copy-start(bf16[128,128]{1,0:T(8,128)(2,1)} %x_ref.1) | copy-start | bytes 98308
  0.7 3.2 %copy-start.4 = (bf16[128,128]{1,0:T(8,128)(2,1)S(1)}, bf16[128,128]{1,0:T(8,128)(2,1)}, u32[]{:S(2)}) copy-start(bf16[128,128]{1,0:T(8,128)(2,1)} %dy_ref.1) | copy-start | bytes 98308
  3.9 1.2 copy-start.1
  5.1 1.2 copy-start.2

commit v6 on v5

--- a/solution.py
+++ b/solution.py
@@ -37,7 +37,7 @@
     out_x, out_c,
     wg_ref, wu_ref, wd_ref,
     raw_dy, raw_x, z_marks, place_ref, x_dy, x_x, l_dy, l_x, x_marks, l_marks, y_marks,
-    pick_ref, rank_ref, row_ref,
+    pick_ref, rank_ref, row_ref, home_ref,
     fan_x, fan_dy, full_x, full_dy, acc_g, acc_u, acc_b, dg_ref, du_ref,
     keep, give, got, pair, back, gate_ref, c_own, c_got, c_all, acc,
     o_x, m_x, h_x, o_c, m_c, s_c, h_c, zo_x,
@@ -60,8 +60,6 @@
     x, z = grp // nz, grp % nz
     y, core = loc // 2, loc % 2
     twin = (grp, 2 * y + 1 - core)
-    my_cols = pl.ds(pl.multiple_of(core * wide, wide), wide)
-    twin_cols = pl.ds(pl.multiple_of((1 - core) * wide, wide), wide)
 
     def rdma(src, dst, ss, rs, to):
         return pltpu.make_async_remote_copy(
@@ -174,9 +172,12 @@
         pass_on(k, away)
     slot_rows = lax.broadcasted_iota(I32, (send, half), 0).astype(F32)
 
+    def chosen_rows(rows):
+        return jnp.concatenate([(row == slot_rows).astype(F32) for row in rows], axis=0)
+
     def place(i, _):
-        parts = [z_marks[pl.ds(i * 8 + xx, 1), :] == slot_rows for xx in range(NX)]
-        place_ref[i] = bits(jnp.concatenate([part.astype(F32) for part in parts], axis=0) > 0.5)
+        rows = [z_marks[pl.ds(i * 8 + xx, 1), :] for xx in range(NX)]
+        place_ref[i] = chosen_rows(rows).astype(BF16)
         return _
 
     lax.fori_loop(0, nz, place, 0)
@@ -301,20 +302,20 @@
     def fan_copy(k, m, slot):
         src, dst = ((fan_dy, full_dy), (fan_x, full_x))[k]
         return rdma(
-            src.at[m], dst.at[slot, :, my_cols], fan_ss.at[m, k], fan_rs.at[slot, k], peer(m)
+            src.at[m], dst.at[slot, core], fan_ss.at[m, k], fan_rs.at[slot, k], peer(m)
         )
 
     def twin_copy(k, slot):
         buf = (full_dy, full_x)[k]
         return rdma(
-            buf.at[slot, :, my_cols], buf.at[slot, :, my_cols],
+            buf.at[slot, core], buf.at[slot, core],
             twin_ss.at[slot, k], twin_rs.at[slot, k], twin,
         )
 
     def twin_arrival(k, slot):
         buf = (full_dy, full_x)[k]
         return rdma(
-            buf.at[slot, :, twin_cols], buf.at[slot, :, twin_cols],
+            buf.at[slot, 1 - core], buf.at[slot, 1 - core],
             twin_ss.at[slot, k], twin_rs.at[slot, k], twin,
         )
 
@@ -344,7 +345,7 @@
 
             @pl.when(i == n - 1)
             def _near():
-                dst[y, :, my_cols] = out
+                dst[y, core] = out
                 twin_copy(k, y).start()
 
             return _
@@ -387,7 +388,8 @@
     def back_rows(slot, _):
         twin_arrival(0, slot).wait_recv()
         acc_b[...] += lax.dot_general(
-            full_dy[slot], wd_ref[:, columns(slot)], NT, preferred_element_type=F32
+            jnp.concatenate([full_dy[slot, 0], full_dy[slot, 1]], axis=1),
+            wd_ref[:, columns(slot)], NT, preferred_element_type=F32
         )
         return _
 
@@ -398,7 +400,7 @@
     def multiply(slot):
         twin_arrival(1, slot).wait_recv()
         rows = columns(slot)
-        xs = full_x[slot]
+        xs = jnp.concatenate([full_x[slot, 0], full_x[slot, 1]], axis=1)
         acc_g[...] += dot(xs, wg_ref[rows, :])
         acc_u[...] += dot(xs, wu_ref[rows, :])
 
@@ -475,12 +477,20 @@
     lane_iota = lax.broadcasted_iota(I32, (lanes, room), 1).astype(F32)
     pick_row = lax.broadcasted_iota(I32, (wide, room), 0)
 
-    def combine(slot):
+    def combine(slot, wait=None):
         rank = dot(rank_ref[...], bits(pick_row == slot))
         pick = bits(rank == lane_iota)
+        if wait is not None:
+            wait.wait_recv()
         acc[...] += dot(pick, back[slot])
 
     combine(y)
+
+    for zz in range(nz):
+        rows = [marks_ref[zz, xx : xx + 1, :] for xx in range(NX)]
+        place_ref[zz] = chosen_rows(rows).astype(BF16)
+    home_place = place_ref[...].astype(F32).reshape(lanes, half).T
+    home_ref[...] = home_place[:tok].astype(BF16)
 
     rdma(c_own, c_got, cx_ss, cx_rs, twin).wait_recv()
     c_lane = dot((c_own[...] + c_got[...]).astype(BF16), pick_ref[y])[:1, :]
@@ -500,8 +510,7 @@
 
     def collect(i, _):
         slot = source(i)
-        ret_copy(slot, slot).wait_recv()
-        combine(slot)
+        combine(slot, ret_copy(slot, slot))
         return _
 
     lax.fori_loop(0, n - 1, collect, 0)
@@ -602,7 +611,7 @@
         return _
 
     lax.fori_loop(0, n - 1, c_in, 0)
-    out_x[...] = h_x[...]
+    out_x[...] = dot(home_ref[...], h_x[...].reshape(lanes, wide)).astype(BF16)
     out_c[...] = c_all[...]
 
     def drain_z(i, _):
@@ -665,12 +674,12 @@
     block = (n, room, wide)
     by_x = (NX, lanes // NX, wide)
     vmem = pl.BlockSpec(memory_space=pltpu.VMEM)
-    hbm = pl.BlockSpec(memory_space=pl.ANY)
+    hbm = pl.BlockSpec(memory_space=pltpu.HBM)
     half = META // 2
     return pl.pallas_call(
         kernel,
         out_shape=(
-            jax.ShapeDtypeStruct(packed, BF16),
+            jax.ShapeDtypeStruct((tok, wide), BF16),
             jax.ShapeDtypeStruct((n, nz, half), F32),
         ),
         in_specs=[vmem] * 3 + [hbm] * 3,
@@ -693,10 +702,11 @@
             pltpu.VMEM((n, room, lanes), BF16),
             pltpu.VMEM((lanes, wide), BF16),
             pltpu.VMEM((8, lanes), F32),
+            pltpu.VMEM((tok, lanes), BF16),
             pltpu.VMEM(block, BF16),
             pltpu.VMEM(block, BF16),
-            pltpu.VMEM((n, room, 2 * wide), BF16),
-            pltpu.VMEM((n, room, 2 * wide), BF16),
+            pltpu.VMEM((n, 2, room, wide), BF16),
+            pltpu.VMEM((n, 2, room, wide), BF16),
             pltpu.VMEM((room, hidden), F32),
             pltpu.VMEM((room, hidden), F32),
             pltpu.VMEM((room, hidden), F32),
@@ -774,18 +784,14 @@
     member = expert_ids % exp_grp
     sent = group_slot < send
     order = group % nz * NX + group // nz
-    lane = jnp.where(sent, order * send + group_slot, lanes)
-    place = jnp.any(
-        lane.T[None] == jnp.arange(lanes, dtype=I32)[:, None, None], axis=1
-    ).astype(BF16)
-    field = jnp.where(sent, member * part + group_slot, exp_grp * part).reshape(-1)
-    of_group = (order.reshape(-1)[None, :] == jnp.arange(n_grp, dtype=I32)[:, None]).astype(BF16)
+    field = jnp.where(sent, member * part + group_slot, exp_grp * part).T.reshape(-1)
+    of_group = (order.T.reshape(-1)[None, :] == jnp.arange(n_grp, dtype=I32)[:, None]).astype(BF16)
     of_field = field[:, None] == jnp.arange(exp_grp * part, dtype=I32)[None, :]
     here = sent & (member == lax.axis_index("loc") // 2)
-    own = jnp.where(here, group_slot, META).reshape(-1)[:, None]
+    own = jnp.where(here, group_slot, META).T.reshape(-1)[:, None]
     own = own == jnp.arange(part, dtype=I32)[None, :]
     marks = dot(
-        of_group, jnp.where(own, gate_probs.reshape(-1)[:, None], jnp.zeros((), BF16))
+        of_group, jnp.where(own, gate_probs.T.reshape(-1)[:, None], jnp.zeros((), BF16))
     ).reshape(nz, 1, META // 2)
     spots = jnp.where(
         (order.T[None] == jnp.arange(n_grp, dtype=I32)[:, None, None]) & sent.T[None],
@@ -795,7 +801,7 @@
     spots = jnp.min(spots, axis=1).astype(F32).reshape(nz, NX, tok)
     spots = jnp.pad(spots, ((0, 0), (0, 0), (0, META // 2 - tok)), constant_values=META)
     meta = jnp.concatenate([spots, marks, jnp.zeros((nz, 7 - NX, META // 2), F32)], axis=1)
-    home_x, home_c = routed(
+    in_grad, home_c = routed(
         inputs,
         out_grad,
         meta,
@@ -806,18 +812,12 @@
         room,
         send,
     )
-    in_grad = lax.dot_general(
-        place,
-        home_x.reshape(lanes, wide),
-        (((0,), (0,)), ((), ())),
-        preferred_element_type=F32,
-    ).astype(BF16)
     table = home_c.reshape(exp_grp, nz, NX, part).transpose(1, 2, 0, 3).reshape(n_grp, -1)
     picks = lax.dot_general(
         of_group, table.astype(BF16), (((0,), (0,)), ((), ())), preferred_element_type=F32
     )
     gate_grad = jnp.sum(jnp.where(of_field, picks, 0.0), axis=1).astype(BF16)
-    return in_grad, gate_grad.reshape(expert_ids.shape)
+    return in_grad, gate_grad.reshape(expert_ids.T.shape).T
 
 
 def solution(mesh):

time: 130 us -> 130 us (level)
  Pallas kernels: 119 us -> 121 us
  local copies, waits for them, and re-layouts: 5.48 us -> 3.55 us
    pallas_call x1, Pallas kernels: 119 us -> 121 us  [routed(): pl.pallas_call(kernel, out_shape=(jax.ShapeDtypeStruct((tok, wide), BF16)...]
    reduce_or x1 -> x0, other arithmetic: 1.32 us -> none  [shards(): jnp.any(lane.T[None] == jnp.arange(lanes, dtype=I32)[:, None, None], axis=1)]
    unnamed x14 -> x11, local copies, waits for them, and re-layouts: 3.96 us -> 3.07 us
where the time goes in v6:
time: 130 us
  Pallas kernels  121 us (93%)
  local copies, waits for them, and re-layouts  3.55 us (3%)
  other arithmetic  2.38 us (2%)
  matrix products  2.22 us (2%)
    pallas_call x1, Pallas kernels, routed(): pl.pallas_call(kernel, out_shape=(jax.ShapeDtypeStruct((tok, wide), BF16)...  121 us
    unnamed x11, local copies, waits for them, and re-layouts  3.07 us

profile of v6, /device:TPU:1, one launch (start us, length us, event | category | flops | bytes accessed | tf_op | source)
XLA Modules:
  0.0 129.7 jit_solution(4476598907550281505)
XLA Ops:
  0.6 0.0 copy-start
  0.6 0.0 copy-start.4
  0.6 0.0 copy-start.3
  0.7 0.1 pad.2.clone
  0.8 0.8 fusion.18
  1.5 0.7 select_bitcast_fusion
  2.3 0.8 select_reduce_fusion
  3.1 1.2 fusion.2
  4.3 0.1 reshape.24
  4.4 0.1 maximum_maximum_fusion.marks_ref
  4.4 0.0 copy-done
  4.4 0.0 copy-done.4
  4.5 0.0 copy-done.3
  4.5 0.0 copy-start.1
  4.5 1.2 copy-done.1
  5.7 0.0 copy-start.2
  5.7 1.2 copy-done.2
  6.9 120.8 %shard_map.95 = (bf16[128,128]{1,0:T(8,128)(2,1)S(1)}, f32[8,16,128]{2,1,0:T(8,128)S(1)}) custom-call(bf16[128,128]{1,0:T(8,128)(2,1)S(1)} %copy-done.3, bf16[128,128]{1,0:T(8,128)(2,1)S(1)} %copy-done.4, f32[16,8,128]{2,1,0:T(8,128)S(1)} %maximum_maximum_fusion.marks_ref, bf16[2048,256]{1,0:T(8,128)(2,1)S(1)} %bitcast.33, bf16[2048,256]{1,0:T(8,128)(2,1)S(1)} %bitcast.34, ...), custom_call_target="tpu_custom_call" | custom-call | flops 1342177280 | bytes 8388608 | tf_op jit(solution)/shard_map/pallas_call | solution.py:679
  127.8 0.1 convert_element_type.30
  127.9 0.1 copy.19
  128.0 0.1 convert_element_type.32
  128.1 1.0 fusion
  129.1 0.6 copy.21
  (3 shorter events, 0.0 us)
Async XLA Ops:
  0.6 3.8 %copy-start = (bf16[1,2048,256]{2,1,0:T(8,128)(2,1)S(1)}, bf16[1,2048,256]{2,1,0:T(8,128)(2,1)}, u32[]{:S(2)}) copy-start(bf16[1,2048,256]{2,1,0:T(8,128)(2,1)} %param.13) | copy-start | bytes 3145732
  0.6 3.8 %copy-start.4 = (bf16[128,128]{1,0:T(8,128)(2,1)S(1)}, bf16[128,128]{1,0:T(8,128)(2,1)}, u32[]{:S(2)}) copy-start(bf16[128,128]{1,0:T(8,128)(2,1)} %dy_ref.1) | copy-start | bytes 98308
  0.6 3.8 %copy-start.3 = (bf16[128,128]{1,0:T(8,128)(2,1)S(1)}, bf16[128,128]{1,0:T(8,128)(2,1)}, u32[]{:S(2)}) copy-start(bf16[128,128]{1,0:T(8,128)(2,1)} %x_ref.1) | copy-start | bytes 98308
  4.5 1.2 copy-start.1
  5.7 1.2 copy-start.2
